TPU v7x, 32 devices: a whole 2x2x4 slice. The times are simulated.
32 devices in a mesh: dp: 8 (over y, x, core), fsdp: 4 (over z).
Axes of the slice: x: 2, y: 2, z: 4, core: 2. Of those that a mesh axis runs over, the one named last changes fastest.
Arguments:
- characters: bfloat16 [32, 512, 16, 256], P(('dp', 'fsdp')), may hold values from -6 to 6
- counts: int32 [32, 512], P(('dp', 'fsdp')), may hold values from 1 to 16
- separators: int32 [32, 512], P(('dp', 'fsdp')), may hold values 0 or 1
- cotangent: bfloat16 [32, 512, 512], P(('dp', 'fsdp')), may hold values from -6 to 6
- char_qkv: bfloat16 [256, 768], P('fsdp', 'dp'), may hold values from -0.375 to 0.375
- char_proj: bfloat16 [256, 256], P('fsdp', 'dp'), may hold values from -0.75 to 0.75
- char_up: bfloat16 [256, 1024], P('fsdp', 'dp'), may hold values from -0.375 to 0.375
- char_down: bfloat16 [1024, 256], P('fsdp', 'dp'), may hold values from -0.1875 to 0.1875
- char_gain_a: bfloat16 [256], P('dp'), may hold values from 0.5 to 1.5
- char_gain_b: bfloat16 [256], P('dp'), may hold values from 0.5 to 1.5
- pool_proj: bfloat16 [256, 512], P('fsdp', 'dp'), may hold values from -1 to 1
- word_qkv: bfloat16 [512, 1536], P('fsdp', 'dp'), may hold values from -0.25 to 0.25
- word_proj: bfloat16 [512, 512], P('fsdp', 'dp'), may hold values from -1 to 1
- word_up: bfloat16 [512, 2048], P('fsdp', 'dp'), may hold values from -0.25 to 0.25
- word_down: bfloat16 [2048, 512], P('fsdp', 'dp'), may hold values from -0.125 to 0.125
- word_gain_a: bfloat16 [512], P('dp'), may hold values from 0.5 to 1.5
- word_gain_b: bfloat16 [512], P('dp'), may hold values from 0.5 to 1.5
Outputs:
- word_out: bfloat16 [32, 512, 512], P(('dp', 'fsdp'))
- char_grad: bfloat16 [32, 512, 16, 256], P(('dp', 'fsdp'))
- grad_char_qkv: float32 [256, 768], P('fsdp', 'dp')
- grad_char_proj: float32 [256, 256], P('fsdp', 'dp')
- grad_char_up: float32 [256, 1024], P('fsdp', 'dp')
- grad_char_down: float32 [1024, 256], P('fsdp', 'dp')
- grad_char_gain_a: float32 [256], P('dp')
- grad_char_gain_b: float32 [256], P('dp')
- grad_pool_proj: float32 [256, 512], P('fsdp', 'dp')
- grad_word_qkv: float32 [512, 1536], P('fsdp', 'dp')
- grad_word_proj: float32 [512, 512], P('fsdp', 'dp')
- grad_word_up: float32 [512, 2048], P('fsdp', 'dp')
- grad_word_down: float32 [2048, 512], P('fsdp', 'dp')
- grad_word_gain_a: float32 [512], P('dp')
- grad_word_gain_b: float32 [512], P('dp')
Inputs may be any that keep to these rules, and one draw needn't show every extreme that they name: Character slots at or past a word's counts are padding. `separators`: 1 marks a word that starts a new document in its row.
All inputs are finite; a program needn't handle non-finite values. No bound on the sum of `separators` on one device may be relied on, other than what follows from the above.
Results may differ from a plain program's by a relative error of at most 0.02.
Values may be sent and summed in bfloat16 or wider, within the bound.
A program may use at most 256 MiB of HBM per device.

v0:
```python
import jax
import jax.numpy as jnp
from jax import lax
from jax.sharding import PartitionSpec as P

CHAR_HEADS = 4
WORD_HEADS = 8


EPS = 1e-05
NEGATIVE = -1e30
tile_rows = 128


def layer_norm(values, gain_vec):
    average = jnp.mean(values, -1, keepdims=True)
    centred = values - average
    spread = jnp.mean(centred * centred, -1, keepdims=True)
    return centred * lax.rsqrt(spread + EPS) * gain_vec


def norm_back(values, gain_vec, upstream):
    unused_out, pullback = jax.vjp(layer_norm, values, gain_vec)
    return pullback(upstream)


def gelu_back(pre_act, upstream):
    unused_out, pullback = jax.vjp(jax.nn.gelu, pre_act)
    return pullback(upstream)[0]


def matmul(left_op, right_op):
    return jnp.dot(left_op, right_op, preferred_element_type=jnp.float32)


def contract_rows(left_op, right_op):
    return lax.dot_general(
        left_op, right_op, (((0,), (0,)), ((), ())), preferred_element_type=jnp.float32
    )


def contract_cols(left_op, right_op):
    return lax.dot_general(
        left_op, right_op, (((1,), (1,)), ((), ())), preferred_element_type=jnp.float32
    )


def masked_scores(queries, key_rows, allowed, factor):
    scores = (
        jnp.einsum("bqhe,bkhe->bhqk", queries, key_rows, preferred_element_type=jnp.float32)
        * factor
    )
    return jnp.where(allowed[:, None], scores, NEGATIVE)


def attend(queries, key_rows, value_rows, allowed, factor):
    scores = masked_scores(queries, key_rows, allowed, factor)
    highest = jnp.max(scores, -1, keepdims=True)
    shifted = jnp.exp(scores - highest)
    totals = jnp.sum(shifted, -1, keepdims=True)
    weights = (shifted / totals).astype(jnp.bfloat16)
    output = jnp.einsum("bhqk,bkhe->bqhe", weights, value_rows, preferred_element_type=jnp.float32)
    return (output.astype(jnp.bfloat16), highest + jnp.log(totals))


def attend_back(queries, key_rows, value_rows, allowed, factor, log_totals, grad_out):
    scores = masked_scores(queries, key_rows, allowed, factor)
    probs_full = jnp.exp(scores - log_totals)
    grad_probs = jnp.einsum(
        "bqhe,bkhe->bhqk", grad_out, value_rows, preferred_element_type=jnp.float32
    )
    grad_values = jnp.einsum(
        "bhqk,bqhe->bkhe",
        probs_full.astype(jnp.bfloat16),
        grad_out,
        preferred_element_type=jnp.float32,
    )
    inner_sum = jnp.sum(probs_full * grad_probs, -1, keepdims=True)
    grad_scores = (probs_full * (grad_probs - inner_sum)).astype(jnp.bfloat16)
    grad_queries = (
        jnp.einsum("bhqk,bkhe->bqhe", grad_scores, key_rows, preferred_element_type=jnp.float32)
        * factor
    )
    grad_keys = (
        jnp.einsum("bhqk,bqhe->bkhe", grad_scores, queries, preferred_element_type=jnp.float32)
        * factor
    )
    return jnp.stack((grad_queries, grad_keys, grad_values), 2)


def gather_char(char_qkv, char_proj, char_up, char_down, pool_proj, char_gain_a, char_gain_b):
    columns = (
        lax.all_gather(char_qkv, "dp", axis=1, tiled=True),
        lax.all_gather(char_proj, "dp", axis=1, tiled=True),
        lax.all_gather(char_up, "dp", axis=1, tiled=True),
        lax.all_gather(char_down, "dp", axis=1, tiled=True),
        lax.all_gather(pool_proj, "dp", axis=1, tiled=True),
        lax.all_gather(char_gain_a, "dp", axis=0, tiled=True),
        lax.all_gather(char_gain_b, "dp", axis=0, tiled=True),
    )
    matrices = (
        lax.all_gather(columns[0], "fsdp", axis=0, tiled=True),
        lax.all_gather(columns[1], "fsdp", axis=0, tiled=True),
        lax.all_gather(columns[2], "fsdp", axis=0, tiled=True),
        lax.all_gather(columns[3], "fsdp", axis=0, tiled=True),
        lax.all_gather(columns[4], "fsdp", axis=0, tiled=True),
    )
    return tuple(matrices) + (columns[5].astype(jnp.float32), columns[6].astype(jnp.float32))


def gather_word(word_qkv, word_proj, word_up, word_down, word_gain_a, word_gain_b):
    columns = (
        lax.all_gather(word_qkv, "dp", axis=1, tiled=True),
        lax.all_gather(word_proj, "dp", axis=1, tiled=True),
        lax.all_gather(word_up, "dp", axis=1, tiled=True),
        lax.all_gather(word_down, "dp", axis=1, tiled=True),
        lax.all_gather(word_gain_a, "dp", axis=0, tiled=True),
        lax.all_gather(word_gain_b, "dp", axis=0, tiled=True),
    )
    matrices = (
        lax.all_gather(columns[0], "fsdp", axis=0, tiled=True),
        lax.all_gather(columns[1], "fsdp", axis=0, tiled=True),
        lax.all_gather(columns[2], "fsdp", axis=0, tiled=True),
        lax.all_gather(columns[3], "fsdp", axis=0, tiled=True),
    )
    return tuple(matrices) + (columns[4].astype(jnp.float32), columns[5].astype(jnp.float32))


def gather_char_again(char_qkv, char_proj, char_up, char_down, pool_proj, char_gain_a, char_gain_b):
    columns = (
        lax.all_gather(char_qkv, "dp", axis=1, tiled=True),
        lax.all_gather(char_proj, "dp", axis=1, tiled=True),
        lax.all_gather(char_up, "dp", axis=1, tiled=True),
        lax.all_gather(char_down, "dp", axis=1, tiled=True),
        lax.all_gather(pool_proj, "dp", axis=1, tiled=True),
        lax.all_gather(char_gain_a, "dp", axis=0, tiled=True),
        lax.all_gather(char_gain_b, "dp", axis=0, tiled=True),
    )
    matrices = (
        lax.all_gather(columns[0], "fsdp", axis=0, tiled=True),
        lax.all_gather(columns[1], "fsdp", axis=0, tiled=True),
        lax.all_gather(columns[2], "fsdp", axis=0, tiled=True),
        lax.all_gather(columns[3], "fsdp", axis=0, tiled=True),
        lax.all_gather(columns[4], "fsdp", axis=0, tiled=True),
    )
    return tuple(matrices) + (columns[5].astype(jnp.float32), columns[6].astype(jnp.float32))


def gather_word_again(word_qkv, word_proj, word_up, word_down, word_gain_a, word_gain_b):
    columns = (
        lax.all_gather(word_qkv, "dp", axis=1, tiled=True),
        lax.all_gather(word_proj, "dp", axis=1, tiled=True),
        lax.all_gather(word_up, "dp", axis=1, tiled=True),
        lax.all_gather(word_down, "dp", axis=1, tiled=True),
        lax.all_gather(word_gain_a, "dp", axis=0, tiled=True),
        lax.all_gather(word_gain_b, "dp", axis=0, tiled=True),
    )
    matrices = (
        lax.all_gather(columns[0], "fsdp", axis=0, tiled=True),
        lax.all_gather(columns[1], "fsdp", axis=0, tiled=True),
        lax.all_gather(columns[2], "fsdp", axis=0, tiled=True),
        lax.all_gather(columns[3], "fsdp", axis=0, tiled=True),
    )
    return tuple(matrices) + (columns[4].astype(jnp.float32), columns[5].astype(jnp.float32))


def shards(
    characters,
    counts,
    separators,
    cotangent,
    char_qkv,
    char_proj,
    char_up,
    char_down,
    char_gain_a,
    char_gain_b,
    pool_proj,
    word_qkv,
    word_proj,
    word_up,
    word_down,
    word_gain_a,
    word_gain_b,
):
    char_weights = gather_char(
        char_qkv, char_proj, char_up, char_down, pool_proj, char_gain_a, char_gain_b
    )
    word_weights = gather_word(word_qkv, word_proj, word_up, word_down, word_gain_a, word_gain_b)
    (
        full_char_qkv,
        full_char_proj,
        full_char_up,
        full_char_down,
        full_pool,
        char_norm_a,
        char_norm_b,
    ) = char_weights
    full_word_qkv, full_word_proj, full_word_up, full_word_down, word_norm_a, word_norm_b = (
        word_weights
    )
    row_count, length, letters, char_width = characters.shape
    word_width = cotangent.shape[2]
    word_count = row_count * length
    char_count = word_count * letters
    blocks = char_count // tile_rows
    char_head = char_width // CHAR_HEADS
    word_head = word_width // WORD_HEADS
    char_factor = char_head ** (-0.5)
    word_factor = word_head ** (-0.5)
    valid_chars = (
        lax.broadcasted_iota(jnp.int32, (row_count, length, letters), 2) < counts[:, :, None]
    )
    slot_word = lax.broadcasted_iota(jnp.int32, (tile_rows, tile_rows), 0) // letters
    other_word = lax.broadcasted_iota(jnp.int32, (tile_rows, tile_rows), 1) // letters
    char_allowed = (slot_word == other_word)[None] & valid_chars.reshape(blocks, 1, tile_rows)
    counts_float = counts.reshape(word_count, 1).astype(jnp.float32)
    chars_flat = characters.reshape(char_count, char_width).astype(jnp.float32)
    normed_a = layer_norm(chars_flat, char_norm_a).astype(jnp.bfloat16)
    char_triple = matmul(normed_a, full_char_qkv).astype(jnp.bfloat16)
    char_split = char_triple.reshape(blocks, tile_rows, 3, CHAR_HEADS, char_head)
    char_att, char_lse = attend(
        char_split[:, :, 0], char_split[:, :, 1], char_split[:, :, 2], char_allowed, char_factor
    )
    char_att = char_att.reshape(char_count, char_width)
    hidden_one = chars_flat + matmul(char_att, full_char_proj)
    normed_b = layer_norm(hidden_one, char_norm_b).astype(jnp.bfloat16)
    char_pre = matmul(normed_b, full_char_up)
    char_act = jax.nn.gelu(char_pre).astype(jnp.bfloat16)
    hidden_two = hidden_one + matmul(char_act, full_char_down)
    summed_chars = jnp.sum(
        jnp.where(
            valid_chars.reshape(word_count, letters, 1),
            hidden_two.reshape(word_count, letters, char_width),
            0.0,
        ),
        1,
    )
    pooled = (summed_chars / counts_float).astype(jnp.bfloat16)
    word_in = matmul(pooled, full_pool)
    documents = jnp.cumsum(separators, 1, dtype=jnp.int32)
    places = lax.broadcasted_iota(jnp.int32, (length, length), 0)
    earlier = lax.broadcasted_iota(jnp.int32, (length, length), 1)
    word_allowed = (earlier <= places)[None] & (documents[:, :, None] == documents[:, None, :])
    normed_c = layer_norm(word_in, word_norm_a).astype(jnp.bfloat16)
    word_triple = matmul(normed_c, full_word_qkv).astype(jnp.bfloat16)
    word_split = word_triple.reshape(row_count, length, 3, WORD_HEADS, word_head)
    word_att, word_lse = attend(
        word_split[:, :, 0], word_split[:, :, 1], word_split[:, :, 2], word_allowed, word_factor
    )
    word_att = word_att.reshape(word_count, word_width)
    hidden_three = word_in + matmul(word_att, full_word_proj)
    normed_d = layer_norm(hidden_three, word_norm_b).astype(jnp.bfloat16)
    word_pre = matmul(normed_d, full_word_up)
    word_act = jax.nn.gelu(word_pre).astype(jnp.bfloat16)
    word_result = hidden_three + matmul(word_act, full_word_down)
    word_out = word_result.astype(jnp.bfloat16).reshape(row_count, length, word_width)
    back_word = gather_word_again(word_qkv, word_proj, word_up, word_down, word_gain_a, word_gain_b)
    back_word_qkv, back_word_proj, back_word_up, back_word_down, back_norm_wa, back_norm_wb = (
        back_word
    )
    upstream = cotangent.reshape(word_count, word_width)
    grad_word_down = contract_rows(word_act, upstream)
    grad_word_act = contract_cols(upstream, back_word_down)
    grad_word_pre = gelu_back(word_pre, grad_word_act).astype(jnp.bfloat16)
    grad_word_up = contract_rows(normed_d, grad_word_pre)
    grad_normed_d = contract_cols(grad_word_pre, back_word_up)
    grad_three_norm, grad_word_gain_b = norm_back(hidden_three, back_norm_wb, grad_normed_d)
    grad_three = upstream.astype(jnp.float32) + grad_three_norm
    grad_three_low = grad_three.astype(jnp.bfloat16)
    grad_word_proj = contract_rows(word_att, grad_three_low)
    grad_word_att = contract_cols(grad_three_low, back_word_proj).astype(jnp.bfloat16)
    grad_word_att = grad_word_att.reshape(row_count, length, WORD_HEADS, word_head)
    grad_word_triple = attend_back(
        word_split[:, :, 0],
        word_split[:, :, 1],
        word_split[:, :, 2],
        word_allowed,
        word_factor,
        word_lse,
        grad_word_att,
    )
    grad_word_triple = grad_word_triple.reshape(word_count, 3 * word_width).astype(jnp.bfloat16)
    grad_word_qkv = contract_rows(normed_c, grad_word_triple)
    grad_normed_c = contract_cols(grad_word_triple, back_word_qkv)
    grad_in_norm, grad_word_gain_a = norm_back(word_in, back_norm_wa, grad_normed_c)
    grad_in_low = (grad_three + grad_in_norm).astype(jnp.bfloat16)
    back_char = gather_char_again(
        char_qkv, char_proj, char_up, char_down, pool_proj, char_gain_a, char_gain_b
    )
    (
        back_char_qkv,
        back_char_proj,
        back_char_up,
        back_char_down,
        back_pool,
        back_norm_ca,
        back_norm_cb,
    ) = back_char
    grad_pool_proj = contract_rows(pooled, grad_in_low)
    grad_pooled = contract_cols(grad_in_low, back_pool) / counts_float
    grad_two = jnp.where(valid_chars.reshape(word_count, letters, 1), grad_pooled[:, None, :], 0.0)
    grad_two = grad_two.reshape(char_count, char_width)
    grad_two_low = grad_two.astype(jnp.bfloat16)
    grad_char_down = contract_rows(char_act, grad_two_low)
    grad_char_act = contract_cols(grad_two_low, back_char_down)
    grad_char_pre = gelu_back(char_pre, grad_char_act).astype(jnp.bfloat16)
    grad_char_up = contract_rows(normed_b, grad_char_pre)
    grad_normed_b = contract_cols(grad_char_pre, back_char_up)
    grad_one_norm, grad_char_gain_b = norm_back(hidden_one, back_norm_cb, grad_normed_b)
    grad_one = grad_two + grad_one_norm
    grad_one_low = grad_one.astype(jnp.bfloat16)
    grad_char_proj = contract_rows(char_att, grad_one_low)
    grad_char_att = contract_cols(grad_one_low, back_char_proj).astype(jnp.bfloat16)
    grad_char_att = grad_char_att.reshape(blocks, tile_rows, CHAR_HEADS, char_head)
    grad_char_triple = attend_back(
        char_split[:, :, 0],
        char_split[:, :, 1],
        char_split[:, :, 2],
        char_allowed,
        char_factor,
        char_lse,
        grad_char_att,
    )
    grad_char_triple = grad_char_triple.reshape(char_count, 3 * char_width).astype(jnp.bfloat16)
    grad_char_qkv = contract_rows(normed_a, grad_char_triple)
    grad_normed_a = contract_cols(grad_char_triple, back_char_qkv)
    grad_chars_norm, grad_char_gain_a = norm_back(chars_flat, back_norm_ca, grad_normed_a)
    char_grad = (grad_one + grad_chars_norm).astype(jnp.bfloat16).reshape(characters.shape)
    gain_totals = lax.psum(
        (grad_char_gain_a, grad_char_gain_b, grad_word_gain_a, grad_word_gain_b), "fsdp"
    )
    row_parts = (
        lax.psum_scatter(
            grad_char_qkv.astype(jnp.bfloat16), "fsdp", scatter_dimension=0, tiled=True
        ).astype(jnp.float32),
        lax.psum_scatter(
            grad_char_proj.astype(jnp.bfloat16), "fsdp", scatter_dimension=0, tiled=True
        ).astype(jnp.float32),
        lax.psum_scatter(
            grad_char_up.astype(jnp.bfloat16), "fsdp", scatter_dimension=0, tiled=True
        ).astype(jnp.float32),
        lax.psum_scatter(
            grad_char_down.astype(jnp.bfloat16), "fsdp", scatter_dimension=0, tiled=True
        ).astype(jnp.float32),
        lax.psum_scatter(
            grad_pool_proj.astype(jnp.bfloat16), "fsdp", scatter_dimension=0, tiled=True
        ).astype(jnp.float32),
        lax.psum_scatter(
            grad_word_qkv.astype(jnp.bfloat16), "fsdp", scatter_dimension=0, tiled=True
        ).astype(jnp.float32),
        lax.psum_scatter(
            grad_word_proj.astype(jnp.bfloat16), "fsdp", scatter_dimension=0, tiled=True
        ).astype(jnp.float32),
        lax.psum_scatter(
            grad_word_up.astype(jnp.bfloat16), "fsdp", scatter_dimension=0, tiled=True
        ).astype(jnp.float32),
        lax.psum_scatter(
            grad_word_down.astype(jnp.bfloat16), "fsdp", scatter_dimension=0, tiled=True
        ).astype(jnp.float32),
    )
    finals = (
        lax.psum_scatter(
            row_parts[0].astype(jnp.bfloat16), "dp", scatter_dimension=1, tiled=True
        ).astype(jnp.float32),
        lax.psum_scatter(
            row_parts[1].astype(jnp.bfloat16), "dp", scatter_dimension=1, tiled=True
        ).astype(jnp.float32),
        lax.psum_scatter(
            row_parts[2].astype(jnp.bfloat16), "dp", scatter_dimension=1, tiled=True
        ).astype(jnp.float32),
        lax.psum_scatter(
            row_parts[3].astype(jnp.bfloat16), "dp", scatter_dimension=1, tiled=True
        ).astype(jnp.float32),
        lax.psum_scatter(
            row_parts[4].astype(jnp.bfloat16), "dp", scatter_dimension=1, tiled=True
        ).astype(jnp.float32),
        lax.psum_scatter(
            row_parts[5].astype(jnp.bfloat16), "dp", scatter_dimension=1, tiled=True
        ).astype(jnp.float32),
        lax.psum_scatter(
            row_parts[6].astype(jnp.bfloat16), "dp", scatter_dimension=1, tiled=True
        ).astype(jnp.float32),
        lax.psum_scatter(
            row_parts[7].astype(jnp.bfloat16), "dp", scatter_dimension=1, tiled=True
        ).astype(jnp.float32),
        lax.psum_scatter(
            row_parts[8].astype(jnp.bfloat16), "dp", scatter_dimension=1, tiled=True
        ).astype(jnp.float32),
        lax.psum_scatter(
            gain_totals[0].astype(jnp.bfloat16), "dp", scatter_dimension=0, tiled=True
        ).astype(jnp.float32),
        lax.psum_scatter(
            gain_totals[1].astype(jnp.bfloat16), "dp", scatter_dimension=0, tiled=True
        ).astype(jnp.float32),
        lax.psum_scatter(
            gain_totals[2].astype(jnp.bfloat16), "dp", scatter_dimension=0, tiled=True
        ).astype(jnp.float32),
        lax.psum_scatter(
            gain_totals[3].astype(jnp.bfloat16), "dp", scatter_dimension=0, tiled=True
        ).astype(jnp.float32),
    )
    return (
        word_out,
        char_grad,
        finals[0],
        finals[1],
        finals[2],
        finals[3],
        finals[9],
        finals[10],
        finals[4],
        finals[5],
        finals[6],
        finals[7],
        finals[8],
        finals[11],
        finals[12],
    )


def solution(mesh):
    placed = (
        P(("dp", "fsdp"), None, None, None),
        P(("dp", "fsdp"), None),
        P(("dp", "fsdp"), None),
        P(("dp", "fsdp"), None, None),
        P("fsdp", "dp"),
        P("fsdp", "dp"),
        P("fsdp", "dp"),
        P("fsdp", "dp"),
        P("dp"),
        P("dp"),
        P("fsdp", "dp"),
        P("fsdp", "dp"),
        P("fsdp", "dp"),
        P("fsdp", "dp"),
        P("fsdp", "dp"),
        P("dp"),
        P("dp"),
    )
    return jax.shard_map(
        shards,
        mesh=mesh,
        in_specs=placed,
        out_specs=(
            P(("dp", "fsdp"), None, None),
            P(("dp", "fsdp"), None, None, None),
            P("fsdp", "dp"),
            P("fsdp", "dp"),
            P("fsdp", "dp"),
            P("fsdp", "dp"),
            P("dp"),
            P("dp"),
            P("fsdp", "dp"),
            P("fsdp", "dp"),
            P("fsdp", "dp"),
            P("fsdp", "dp"),
            P("fsdp", "dp"),
            P("dp"),
            P("dp"),
        ),
        check_vma=False,
    )
```

profile of v0, /device:TPU:0, one launch (start us, length us, event | category | flops | bytes accessed | tf_op | source)
XLA Modules:
  0.0 1208.8 jit_solution(8655278554787247086)
XLA Ops:
  7.4 13.0 %all_gather.101 = bf16[128,1536]{0,1:T(8,128)(2,1)} all-gather(bf16[128,192]{0,1:T(8,128)(2,1)} %param.28), channel_id=1, replica_groups=mesh['dp'=8,'fsdp'=4] {'dp'}, dimensions={1}, use_global_device_ids=true | all-gather | bytes 442368 | tf_op jit(solution)/shard_map/all_gather | solution.py:113
  56.2 13.2 %all-reduce.10 = (bf16[256]{0:T(256)(128)(2,1)S(1)}, bf16[256]{0:T(256)(128)(2,1)S(1)}, bf16[512]{0:T(512)(128)(2,1)S(1)}, bf16[512]{0:T(512)(128)(2,1)S(1)}) all-reduce(bf16[256]{0:T(256)(128)(2,1)S(1)} %dynamic-update-slice, bf16[256]{0:T(256)(128)(2,1)S(1)} %dynamic-update-slice.1, ...), channel_id=1, replica_groups=mesh['dp'=8,'fsdp'=4] {'dp'}, use_global_device_ids=true, to_apply=%add | all-reduce | flops 1536 | bytes 6144
  79.6 14.5 %all_gather.92 = bf16[256,256]{1,0:T(8,128)(2,1)S(1)} all-gather(bf16[64,256]{1,0:T(8,128)(2,1)S(1)} %copy.119), channel_id=1, replica_groups=mesh['dp'=8,'fsdp'=4] {'fsdp'}, dimensions={0}, use_global_device_ids=true | all-gather | bytes 163840 | tf_op jit(solution)/shard_map/all_gather | solution.py:103
  138.3 17.3 %all_gather.99 = bf16[256,512]{1,0:T(8,128)(2,1)} all-gather(bf16[64,512]{1,0:T(8,128)(2,1)S(1)} %copy.121), channel_id=1, replica_groups=mesh['dp'=8,'fsdp'=4] {'fsdp'}, dimensions={0}, use_global_device_ids=true | all-gather | bytes 327680 | tf_op jit(solution)/shard_map/all_gather | solution.py:106
  156.9 14.6 %all_gather.90 = bf16[256,768]{1,0:T(8,128)(2,1)S(1)} all-gather(bf16[64,768]{1,0:T(8,128)(2,1)S(1)} %bitcast.269), channel_id=1, replica_groups=mesh['dp'=8,'fsdp'=4] {'fsdp'}, dimensions={0}, use_global_device_ids=true | all-gather | bytes 491520 | tf_op jit(solution)/shard_map/all_gather | solution.py:102
  171.5 14.9 %all_gather.104 = bf16[512,512]{0,1:T(8,128)(2,1)S(1)} all-gather(bf16[128,512]{0,1:T(8,128)(2,1)S(1)} %all_gather.103), channel_id=1, replica_groups=mesh['dp'=8,'fsdp'=4] {'fsdp'}, dimensions={0}, use_global_device_ids=true | all-gather | bytes 655360 | tf_op jit(solution)/shard_map/all_gather | solution.py:122
  186.4 15.9 %all_gather.97 = bf16[1024,256]{0,1:T(8,128)(2,1)S(1)} all-gather(bf16[256,256]{0,1:T(8,128)(2,1)S(1)} %all_gather.96), channel_id=1, replica_groups=mesh['dp'=8,'fsdp'=4] {'fsdp'}, dimensions={0}, use_global_device_ids=true | all-gather | bytes 655360 | tf_op jit(solution)/shard_map/all_gather | solution.py:105
  202.3 15.0 %all_gather.95 = bf16[256,1024]{1,0:T(8,128)(2,1)S(1)} all-gather(bf16[64,1024]{1,0:T(8,128)(2,1)S(1)} %all_gather.94), channel_id=1, replica_groups=mesh['dp'=8,'fsdp'=4] {'fsdp'}, dimensions={0}, use_global_device_ids=true | all-gather | bytes 655360 | tf_op jit(solution)/shard_map/all_gather | solution.py:104
  234.5 36.0 %reshape.617 = bf16[64,128,3,4,64]{4,3,2,1,0:T(4,128)(2,1)} reshape(bf16[8192,768]{1,0:T(8,128)(2,1)} %convolution_convert_fusion) | data formatting | bytes 25165824 | tf_op jit(solution)/shard_map/reshape | solution.py:221
  270.5 20.0 %fusion.96 = (bf16[64,128,1,4,64]{4,3,2,1,0:T(4,128)(2,1)}, bf16[64,128,1,4,64]{4,3,2,1,0:T(4,128)(2,1)}, bf16[64,128,1,4,64]{4,3,2,1,0:T(4,128)(2,1)}) fusion(bf16[64,128,3,4,64]{4,3,2,1,0:T(4,128)(2,1)} %reshape.617), kind=kLoop, calls=%fused_computation.184 | loop fusion | bytes 25165824 | tf_op jit(solution)/shard_map/slice | solution.py:223
  380.9 15.3 %fusion.93 = f32[8192,1024]{1,0:T(8,128)} fusion(bf16[256,1024]{1,0:T(8,128)(2,1)S(1)} %all_gather.95, f32[8192,256]{1,0:T(8,128)} %copy-done, f32[256]{0:T(256)S(1)} %convert_element_type.258, f32[8192]{0:T(1024)S(1)} %fusion.85, f32[8192]{0:T(1024)S(1)} %broadcast_multiply_fusion.1), kind=kOutput, calls=%fused_computation.181 | convolution fusion | flops 4303355904 | bytes 42533888 | tf_op jit(solution)/shard_map/dot_general | solution.py:33
  396.3 18.2 %select_reduce_fusion = f32[512,256]{1,0:T(8,128)S(1)} fusion(pred[512,16]{1,0:T(8,128)(4,1)S(1)} %iota_compare_fusion.1, f32[8192,256]{1,0:T(8,128)} %copy-done, bf16[1024,256]{0,1:T(8,128)(2,1)S(1)} %all_gather.97, f32[8192,1024]{1,0:T(8,128)} %fusion.93), kind=kOutput, calls=%fused_computation.51 | convolution fusion | flops 4376625152 | bytes 42999808 | tf_op jit(solution)/shard_map/dot_general | solution.py:33
  461.8 28.2 %fusion.6 = bf16[8192,1024]{1,0:T(8,128)(2,1)} fusion(f32[8192,1024]{1,0:T(8,128)} %fusion.93, bf16[8192,256]{1,0:T(8,128)(2,1)S(1)} %fusion.18, bf16[1024,256]{0,1:T(8,128)(2,1)S(1)} %copy-done.24), kind=kOutput, calls=%fused_computation.8 | convolution fusion | flops 4462739456 | bytes 55050240 | tf_op jit(solution)/shard_map/dot_general | solution.py:43
  490.1 15.0 %multiply_reduce_fusion.1 = (f32[256]{0:T(256)}, f32[8192]{0:T(1024)S(1)}, f32[8192,256]{1,0:T(8,128)}) fusion(f32[8192,256]{1,0:T(8,128)S(1)} %bitcast.236, f32[8192]{0:T(1024)S(1)} %copy-done.37, f32[8192]{0:T(1024)S(1)} %copy-done.33, f32[256]{0:T(256)S(1)} %copy-done.67, bf16[8192,1024]{1,0:T(8,128)(2,1)} %fusion.6, bf16[256,1024]{1,0:T(8,128)(2,1)S(1)} %copy-done.22), kind=kOutput, calls=%fused_computation.36 | convolution fusion | flops 4309639168 | bytes 34179072 | tf_op jit(solution)/shard_map/dot_general | solution.py:43
  554.8 14.9 %fusion.53 = bf16[64,128,1,4,64]{1,4,3,0,2:T(8,128)(2,1)} fusion(bf16[64,128,4,64]{1,3,2,0:T(8,128)(2,1)} %copy.130, f32[64,4,128,128]{2,3,1,0:T(8,128)} %get-tuple-element.107, f32[64,4,128]{2,1,0:T(4,128)S(1)} %bitcast.253), kind=kOutput, calls=%fused_computation.89 | convolution fusion | flops 545259520 | bytes 25296896 | tf_op jit(solution)/shard_map/bhqk,bqhe->bkhe/dot_general | solution.py:72
  569.7 15.0 %multiply_reduce_fusion = (f32[64,4,128]{2,1,0:T(4,128)S(1)}, f32[64,4,128,128]{2,3,1,0:T(8,128)}) fusion(f32[64,4,128,128]{2,3,1,0:T(8,128)} %get-tuple-element.107, f32[64,4,128]{2,1,0:T(4,128)S(1)} %bitcast.254, bf16[64,128,4,64]{1,3,2,0:T(8,128)(2,1)} %copy.130, bf16[64,128,1,4,64]{1,4,3,0,2:T(8,128)(2,1)} %copy.171), kind=kOutput, calls=%fused_computation.12 | convolution fusion | flops 549421056 | bytes 42205184 | tf_op jit(solution)/shard_map/bqhe,bkhe->bhqk/dot_general | solution.py:69
  631.1 19.1 %fusion.65 = bf16[256,768]{1,0:T(8,128)(2,1)} fusion(bf16[8192,256]{1,0:T(8,128)(2,1)} %bitcast.251, bf16[96,8,64,128]{3,2,1,0:T(8,128)(2,1)} %bitcast.242), kind=kOutput, calls=%fused_computation.111 | convolution fusion | flops 3221422080 | bytes 17170432 | tf_op jit(solution)/shard_map/dot_general | solution.py:37
  651.9 20.8 %convolution_convert_fusion.8 = bf16[1024,256]{1,0:T(8,128)(2,1)} fusion(bf16[8192,256]{1,0:T(8,128)(2,1)} %copy-done.19, f32[8192,1024]{1,0:T(8,128)} %fusion.93), kind=kOutput, calls=%fused_computation.109 | convolution fusion | flops 4370726912 | bytes 38273024 | tf_op jit(solution)/shard_map/dot_general | solution.py:37
  672.8 13.6 %convolution_convert_fusion.9 = bf16[256,1024]{1,0:T(8,128)(2,1)} fusion(bf16[8192,1024]{1,0:T(8,128)(2,1)} %fusion.6, f32[8192,256]{1,0:T(8,128)} %copy-done, f32[256]{0:T(256)S(1)} %copy-done.67, f32[8192]{0:T(1024)S(1)} %copy-done.37, f32[8192]{0:T(1024)S(1)} %copy-done.33), kind=kOutput, calls=%fused_computation.110 | convolution fusion | flops 4303618048 | bytes 25756672 | tf_op jit(solution)/shard_map/dot_general | solution.py:37
  720.2 21.2 %reduce-scatter.39.cloned.1.call-done = bf16[64,1024]{1,0:T(8,128)(2,1)} async-done(((bf16[256,1024]{1,0:T(8,128)(2,1)}), bf16[64,1024]{1,0:T(8,128)(2,1)}) %reduce-scatter.39.cloned.1.call-update) | async-done | bytes 131088 | tf_op jit(solution)/shard_map/reduce_scatter | solution.py:340
  744.4 32.7 %reduce-scatter.45.cloned.1.call-done = bf16[128,1536]{1,0:T(8,128)(2,1)} async-done(((bf16[512,1536]{1,0:T(8,128)(2,1)}), bf16[128,1536]{1,0:T(8,128)(2,1)}) %reduce-scatter.45.cloned.1.call-update) | async-done | bytes 393232 | tf_op jit(solution)/shard_map/reduce_scatter | solution.py:349
  779.2 15.6 %multiply_reduce_fusion.3 = (f32[8192]{0:T(1024)S(1)}, f32[8192,256]{1,0:T(8,128)}) fusion(bf16[1,512,16,256]{3,2,1,0:T(8,128)(2,1)} %param.17, f32[256]{0:T(256)S(1)} %copy-done.79, f32[8192]{0:T(1024)S(1)} %copy-done.41, bf16[256,768]{1,0:T(8,128)(2,1)S(1)} %copy-done.31, bf16[96,8,64,128]{3,2,1,0:T(8,128)(2,1)} %bitcast.243), kind=kOutput, calls=%fused_computation.40 | convolution fusion | flops 3231703040 | bytes 25625600 | tf_op jit(solution)/shard_map/dot_general | solution.py:43
  794.8 27.6 %reduce-scatter.53.cloned.1.call-done = bf16[512,512]{1,0:T(8,128)(2,1)} async-done(((bf16[2048,512]{1,0:T(8,128)(2,1)}), bf16[512,512]{1,0:T(8,128)(2,1)}) %reduce-scatter.53.cloned.1.call-update) | async-done | bytes 524304 | tf_op jit(solution)/shard_map/reduce_scatter | solution.py:358
  833.8 34.6 %reduce-scatter.49.cloned.1.call-done = bf16[128,2048]{1,0:T(8,128)(2,1)} async-done(((bf16[512,2048]{1,0:T(8,128)(2,1)}), bf16[128,2048]{1,0:T(8,128)(2,1)}) %reduce-scatter.49.cloned.1.call-update) | async-done | bytes 524304 | tf_op jit(solution)/shard_map/reduce_scatter | solution.py:355
  911.5 30.1 %reduce-scatter.63.cloned.1.call-done = bf16[64,64]{1,0:T(8,128)(2,1)} async-done(((bf16[512,64]{1,0:T(8,128)(2,1)}), bf16[64,64]{1,0:T(8,128)(2,1)}) %reduce-scatter.63.cloned.1.call-update) | async-done | bytes 8208
  943.0 35.3 %reduce-scatter.55.cloned.1.call-done = bf16[96,64]{1,0:T(8,128)(2,1)} async-done(((bf16[768,64]{1,0:T(8,128)(2,1)}), bf16[96,64]{1,0:T(8,128)(2,1)}) %reduce-scatter.55.cloned.1.call-update) | async-done | bytes 12304
  979.8 34.8 %reduce-scatter.67.cloned.1.call-done = bf16[64,128]{1,0:T(8,128)(2,1)} async-done(((bf16[512,128]{1,0:T(8,128)(2,1)}), bf16[64,128]{1,0:T(8,128)(2,1)}) %reduce-scatter.67.cloned.1.call-update) | async-done | bytes 16400
  1016.1 35.6 %reduce-scatter.61.cloned.1.call-done = bf16[32,256]{1,0:T(8,128)(2,1)} async-done(((bf16[256,256]{1,0:T(8,128)(2,1)}), bf16[32,256]{1,0:T(8,128)(2,1)}) %reduce-scatter.61.cloned.1.call-update) | async-done | bytes 16400
  1053.2 35.0 %reduce-scatter.59.cloned.1.call-done = bf16[128,64]{1,0:T(8,128)(2,1)} async-done(((bf16[1024,64]{1,0:T(8,128)(2,1)}), bf16[128,64]{1,0:T(8,128)(2,1)}) %reduce-scatter.59.cloned.1.call-update) | async-done | bytes 16400
  1089.7 35.8 %reduce-scatter.65.cloned.1.call-done = bf16[192,128]{1,0:T(8,128)(2,1)} async-done(((bf16[1536,128]{1,0:T(8,128)(2,1)}), bf16[192,128]{1,0:T(8,128)(2,1)}) %reduce-scatter.65.cloned.1.call-update) | async-done | bytes 49168
  1127.1 35.7 %reduce-scatter.69.cloned.1.call-done = bf16[64,512]{1,0:T(8,128)(2,1)} async-done(((bf16[512,512]{1,0:T(8,128)(2,1)}), bf16[64,512]{1,0:T(8,128)(2,1)}) %reduce-scatter.69.cloned.1.call-update) | async-done | bytes 65552
  1164.5 35.5 %reduce-scatter.51.cloned.1.call-done = bf16[128,256]{1,0:T(8,128)(2,1)} async-done(((bf16[128,2048]{1,0:T(8,128)(2,1)}), bf16[128,256]{1,0:T(8,128)(2,1)}) %reduce-scatter.51.cloned.1.call-update) | async-done | bytes 65552 | tf_op jit(solution)/shard_map/reduce_scatter | solution.py:384
  (407 shorter events, 445.8 us)
Async XLA Ops:
  7.2 148.6 %copy-start.72 = (s32[1,512]{1,0:T(1,128)S(1)}, s32[1,512]{1,0:T(1,128)}, u32[]{:S(2)}) copy-start(s32[1,512]{1,0:T(1,128)} %param.18) | copy-start | bytes 6148
  7.3 121.8 %copy-start.76 = (bf16[128,64]{0,1:T(8,128)(2,1)S(1)}, bf16[128,64]{0,1:T(8,128)(2,1)}, u32[]{:S(2)}) copy-start(bf16[128,64]{0,1:T(8,128)(2,1)} %param.29) | copy-start | bytes 49156
  7.3 408.7 %all-gather.5.cloned.1.call-start = ((), (), s32[]{:S(2)}) async-start(), calls=%async_computation.18 | async-start | bytes 1966080 | tf_op jit(solution)/shard_map/all_gather | solution.py:121
  20.4 407.4 %all-gather.7.cloned.1.call-start = ((), (), s32[]{:S(2)}) async-start(), calls=%async_computation.19 | async-start | bytes 2621440 | tf_op jit(solution)/shard_map/all_gather | solution.py:123
  33.3 399.6 %all-gather.9.cloned.1.call-start = ((), (), s32[]{:S(2)}) async-start(), calls=%async_computation.20 | async-start | bytes 2621440 | tf_op jit(solution)/shard_map/all_gather | solution.py:124
  44.1 654.9 %reduce-scatter.37.cloned.1.call-start = ((), (), s32[]{:S(2)}) async-start(), calls=%async_computation.22 | async-start | bytes 163840 | tf_op jit(solution)/shard_map/reduce_scatter | solution.py:337
  44.9 412.7 %copy-start.85 = (f32[512]{0:T(512)}, f32[512]{0:T(512)S(1)}, u32[]{:S(2)}) copy-start(f32[512]{0:T(512)S(1)} %convert_element_type.261) | copy-start | bytes 6148
  49.2 176.3 %copy-start.40 = (f32[8192]{0:T(1024)}, f32[8192]{0:T(1024)S(1)}, u32[]{:S(2)}) copy-start(f32[8192]{0:T(1024)S(1)} %div.126) | copy-start | bytes 98308
  69.4 158.7 %copy-start.78 = (f32[256]{0:T(256)}, f32[256]{0:T(256)S(1)}, u32[]{:S(2)}) copy-start(f32[256]{0:T(256)S(1)} %convert_element_type.252) | copy-start | bytes 3076
  69.4 311.5 %copy-start.66 = (f32[256]{0:T(256)}, f32[256]{0:T(256)S(1)}, u32[]{:S(2)}) copy-start(f32[256]{0:T(256)S(1)} %convert_element_type.258) | copy-start | bytes 3076
  69.4 387.7 %copy-start.68 = (f32[512]{0:T(512)}, f32[512]{0:T(512)S(1)}, u32[]{:S(2)}) copy-start(f32[512]{0:T(512)S(1)} %convert_element_type.263) | copy-start | bytes 6148
  69.4 371.9 %copy-start.64 = (f32[512]{0:T(512)}, f32[512]{0:T(512)S(1)}, u32[]{:S(2)}) copy-start(f32[512]{0:T(512)S(1)} %convert_element_type.270) | copy-start | bytes 6148
  94.1 270.7 %copy-start.34 = (bf16[256,256]{1,0:T(8,128)(2,1)}, bf16[256,256]{1,0:T(8,128)(2,1)S(1)}, u32[]{:S(2)}) copy-start(bf16[256,256]{1,0:T(8,128)(2,1)S(1)} %all_gather.92) | copy-start | bytes 393220
  202.3 193.9 %copy-start.23 = (bf16[1024,256]{0,1:T(8,128)(2,1)}, bf16[1024,256]{0,1:T(8,128)(2,1)S(1)}, u32[]{:S(2)}) copy-start(bf16[1024,256]{0,1:T(8,128)(2,1)S(1)} %all_gather.97) | copy-start | bytes 1572868
  217.3 163.6 %copy-start.21 = (bf16[256,1024]{1,0:T(8,128)(2,1)}, bf16[256,1024]{1,0:T(8,128)(2,1)S(1)}, u32[]{:S(2)}) copy-start(bf16[256,1024]{1,0:T(8,128)(2,1)S(1)} %all_gather.95) | copy-start | bytes 1572868
  613.9 86.7 %reduce-scatter.43.cloned.1.call-start = ((), (), s32[]{:S(2)}) async-start(), calls=%async_computation.25 | async-start | bytes 327680 | tf_op jit(solution)/shard_map/reduce_scatter | solution.py:346
  630.9 71.5 %reduce-scatter.35.cloned.1.call-start = ((), (), s32[]{:S(2)}) async-start(), calls=%async_computation.21 | async-start | bytes 491520 | tf_op jit(solution)/shard_map/reduce_scatter | solution.py:334
  650.2 54.0 %reduce-scatter.47.cloned.1.call-start = ((), (), s32[]{:S(2)}) async-start(), calls=%async_computation.27 | async-start | bytes 655360 | tf_op jit(solution)/shard_map/reduce_scatter | solution.py:352
  651.8 66.6 %reduce-scatter.41.cloned.1.call-start = ((), (), s32[]{:S(2)}) async-start(), calls=%async_computation.24 | async-start | bytes 655360 | tf_op jit(solution)/shard_map/reduce_scatter | solution.py:343
  672.7 68.6 %reduce-scatter.39.cloned.1.call-start = ((), (), s32[]{:S(2)}) async-start(), calls=%async_computation.23 | async-start | bytes 655360 | tf_op jit(solution)/shard_map/reduce_scatter | solution.py:340
  686.4 90.7 %reduce-scatter.45.cloned.1.call-start = ((), (), s32[]{:S(2)}) async-start(), calls=%async_computation.26 | async-start | bytes 1966080 | tf_op jit(solution)/shard_map/reduce_scatter | solution.py:349
  688.8 133.6 %reduce-scatter.53.cloned.1.call-start = ((), (), s32[]{:S(2)}) async-start(), calls=%async_computation.30 | async-start | bytes 2621440 | tf_op jit(solution)/shard_map/reduce_scatter | solution.py:358
  694.4 174.0 %reduce-scatter.49.cloned.1.call-start = ((), (), s32[]{:S(2)}) async-start(), calls=%async_computation.28 | async-start | bytes 2621440 | tf_op jit(solution)/shard_map/reduce_scatter | solution.py:355
  699.0 211.0 %reduce-scatter.57.cloned.1.call-start = ((), (), s32[]{:S(2)}) async-start(), calls=%async_computation.32 | async-start | bytes 73728
  700.6 241.0 %reduce-scatter.63.cloned.1.call-start = ((), (), s32[]{:S(2)}) async-start(), calls=%async_computation.35 | async-start | bytes 147456
  702.3 276.0 %reduce-scatter.55.cloned.1.call-start = ((), (), s32[]{:S(2)}) async-start(), calls=%async_computation.31 | async-start | bytes 221184
  704.1 310.4 %reduce-scatter.67.cloned.1.call-start = ((), (), s32[]{:S(2)}) async-start(), calls=%async_computation.37 | async-start | bytes 147456
  705.9 345.8 %reduce-scatter.61.cloned.1.call-start = ((), (), s32[]{:S(2)}) async-start(), calls=%async_computation.34 | async-start | bytes 147456
  720.1 368.1 %reduce-scatter.59.cloned.1.call-start = ((), (), s32[]{:S(2)}) async-start(), calls=%async_computation.33 | async-start | bytes 294912
  743.1 382.3 %reduce-scatter.65.cloned.1.call-start = ((), (), s32[]{:S(2)}) async-start(), calls=%async_computation.36 | async-start | bytes 442368
  779.1 383.7 %reduce-scatter.69.cloned.1.call-start = ((), (), s32[]{:S(2)}) async-start(), calls=%async_computation.38 | async-start | bytes 589824
  824.5 375.6 %reduce-scatter.51.cloned.1.call-start = ((), (), s32[]{:S(2)}) async-start(), calls=%async_computation.29 | async-start | bytes 589824 | tf_op jit(solution)/shard_map/reduce_scatter | solution.py:384
  (87 other events, 2132.8 us)
Sparse Core Ops, SparseCore 0:
  20.5 37.9 all-gather.4
  60.1 46.1 all-gather.6
  108.0 48.9 all-gather.8
  614.0 18.8 reduce-scatter.36
  635.1 17.7 reduce-scatter.42
  655.0 18.7 reduce-scatter.34
  676.2 19.8 reduce-scatter.46
  698.5 19.8 reduce-scatter.40
  721.4 19.8 reduce-scatter.38
  743.6 33.4 reduce-scatter.44
  779.5 42.8 reduce-scatter.52
  825.1 43.1 reduce-scatter.48
  872.2 32.5 reduce-scatter.56
  908.2 33.3 reduce-scatter.62
  944.8 33.4 reduce-scatter.54
  981.2 33.3 reduce-scatter.66
  1018.3 33.3 reduce-scatter.60
  1054.5 33.6 reduce-scatter.58
  1091.5 33.8 reduce-scatter.64
  1128.6 34.1 reduce-scatter.68
  1165.9 34.1 reduce-scatter.50
where the time goes:
time: 1220 us; the launch traced here: 1210 us
  waiting for transfers between devices  407 us (33%)
  matrix products  292 us (24%)
  blocking collectives  216 us (18%)
  local copies, waits for them, and re-layouts  177 us (15%)
  other arithmetic  96.5 us (8%)
  between operations  19.1 us (2%)
    unnamed x29, waiting for transfers between devices  243 us
    unnamed x233, local copies, waits for them, and re-layouts  80.3 us
    dot_general x9, matrix products, contract_cols(): lax.dot_general(left_op, right_op, (((1,), (1,)), ((), ())), preferred_el...  74.6 us
    dot_general x9, matrix products, contract_rows(): lax.dot_general(left_op, right_op, (((0,), (0,)), ((), ())), preferred_el...  71.1 us
    dot_general x9, matrix products, matmul(): return jnp.dot(left_op, right_op, preferred_element_type=jnp.float32)  64.6 us
    reshape x1, local copies, waits for them, and re-layouts, shards(): char_triple.reshape(blocks, tile_rows, 3, CHAR_HEADS, char_head)  36 us
    reduce_scatter x1, waiting for transfers between devices, shards(): lax.psum_scatter(row_parts[7].astype(jnp.bfloat16), 'dp', scatter_dimensi...  35.5 us
    reduce_scatter x1, waiting for transfers between devices, shards(): lax.psum_scatter(grad_word_up.astype(jnp.bfloat16), 'fsdp', scatter_dimen...  34.6 us
  transfers between devices with their start and end apart: 21, of which 13 were waited for; matrix products, arithmetic and copies ran while one was open for 31% of the time, Pallas kernels for 0%

commit v1 on v0

v1 whole, which is shorter than its diff:
```python
import functools

import jax
import jax.numpy as jnp
from jax import lax
from jax.experimental import pallas as pl
from jax.experimental.pallas import tpu as pltpu
from jax.sharding import PartitionSpec as P

CHAR_HEADS = 4
WORD_HEADS = 8
EPS = 1e-05
NEGATIVE = -1e30
LANES = 128
SPAN = 256
STEP = 512
GELU_A = 0.7978845608028654
GELU_B = 0.044715

bf16 = jnp.bfloat16
f32 = jnp.float32


def dot(a, b):
    return jnp.dot(a, b, preferred_element_type=f32)


def dot_nt(a, b):
    return lax.dot_general(a, b, (((1,), (1,)), ((), ())), preferred_element_type=f32)


def normed(v):
    c = v - jnp.mean(v, 0, keepdims=True)
    rs = lax.rsqrt(jnp.mean(c * c, 0, keepdims=True) + EPS)
    return c * rs, rs


def wide(g, n):
    return g if n == g.shape[1] else jnp.concatenate([g] * (n // g.shape[1]), 1)


def gelu_both(u):
    s = u * u
    t = jnp.tanh(u * (GELU_A + (GELU_A * GELU_B) * s))
    h = 0.5 * u
    r = 0.5 + 0.5 * t
    slope = r + h * (1.0 - t * t) * (GELU_A + (3.0 * GELU_A * GELU_B) * s)
    return u * r, slope


def lane_word(letters):
    return lax.broadcasted_iota(jnp.int32, (letters, LANES), 1) // letters


def pick_own(full, owner, letters):
    words = LANES // letters
    out = full[:letters]
    for w in range(1, words):
        out = jnp.where(owner == w, full[w * letters : (w + 1) * letters], out)
    return out


def own_blocks(letters):
    a = lax.broadcasted_iota(jnp.int32, (LANES, LANES), 0) // letters
    b = lax.broadcasted_iota(jnp.int32, (LANES, LANES), 1) // letters
    return jnp.where(a == b, 1.0, 0.0).astype(bf16)


def spread_own(compact, blocks, letters):
    return jnp.concatenate([compact] * (LANES // letters), 0) * blocks


def char_forward_kernel(
    letters, x_ref, tok_ref, cnt_ref, ga_ref, gb_ref, wqkv_ref, wproj_ref, wup_ref, wdown_ref,
    t_ref, o_ref, p_ref, z1_ref, rs1_ref, z2_ref, rs2_ref, m_ref, gp_ref, pool_ref,
):
    step = pl.program_id(0)
    width = x_ref.shape[1]
    head = width // CHAR_HEADS
    scale = head ** (-0.5)
    steps_per_block = LANES * letters // STEP
    owner = lane_word(letters)
    blocks = own_blocks(letters)
    key_slot = lax.broadcasted_iota(jnp.int32, (letters, LANES), 0)

    @pl.when(step % steps_per_block == 0)
    def _():
        pool_ref[...] = jnp.zeros_like(pool_ref)

    for part in range(STEP // SPAN):
        at = pl.ds(part * SPAN, SPAN)
        x = x_ref[at, :].astype(f32).T
        z1, rs1 = normed(x)
        z1_ref[0, :, at] = z1.astype(bf16)
        rs1_ref[0, :, at] = rs1
        a1 = (z1 * wide(ga_ref[...], SPAN)).astype(bf16)
        for n in range(3):
            rows = pl.ds(n * width, width)
            t_ref[0, rows, at] = dot(wqkv_ref[rows, :], a1).astype(bf16)
        for g in range(SPAN // LANES):
            lanes = pl.ds(part * SPAN + g * LANES, LANES)
            allowed = key_slot < tok_ref[0, :, lanes]
            for h in range(CHAR_HEADS):
                q = t_ref[0, pl.ds(h * head, head), lanes]
                k = t_ref[0, pl.ds(width + h * head, head), lanes]
                v = t_ref[0, pl.ds(2 * width + h * head, head), lanes]
                full = dot(k.T, q)
                s = jnp.where(allowed, pick_own(full, owner, letters) * scale, NEGATIVE)
                e = jnp.exp(s - jnp.max(s, 0, keepdims=True))
                p = e / jnp.sum(e, 0, keepdims=True)
                p_ref[0, pl.ds(h * letters, letters), lanes] = p
                o = dot(v, spread_own(p.astype(bf16), blocks, letters))
                o_ref[0, pl.ds(h * head, head), lanes] = o.astype(bf16)
        h1 = x + dot(wproj_ref[...], o_ref[0, :, at])
        z2, rs2 = normed(h1)
        z2_ref[0, :, at] = z2.astype(bf16)
        rs2_ref[0, :, at] = rs2
        a2 = (z2 * wide(gb_ref[...], SPAN)).astype(bf16)
        for n in range(wup_ref.shape[0] // 256):
            rows = pl.ds(n * 256, 256)
            m, gp = gelu_both(dot(wup_ref[rows, :], a2))
            m_ref[0, rows, at] = m.astype(bf16)
            gp_ref[0, rows, at] = gp.astype(bf16)
        h2 = h1 + dot(wdown_ref[...], m_ref[0, :, at])
        high = h2.astype(bf16)
        low = (h2 - high.astype(f32)).astype(bf16)
        row = lax.broadcasted_iota(jnp.int32, (SPAN, LANES), 0)
        word = lax.broadcasted_iota(jnp.int32, (SPAN, LANES), 1)
        first = (step % steps_per_block) * (STEP // letters) + part * (SPAN // letters)
        mine = (row // letters + first == word) & (row % letters < cnt_ref[...])
        gather = jnp.where(mine, 1.0, 0.0).astype(bf16)
        pool_ref[...] += dot(high, gather) + dot(low, gather)


def full_spec(a):
    nd = len(a.shape)
    return pl.BlockSpec(a.shape, lambda i: (0,) * nd)


def char_forward(x, tok, cnt, ga, gb, wqkv_t, wproj_t, wup_t, wdown_t, letters):
    tokens, width = x.shape
    steps = tokens // STEP
    hidden = wup_t.shape[0]
    per = LANES * letters // STEP

    def strip(rows, dtype=bf16):
        return (
            jax.ShapeDtypeStruct((steps, rows, STEP), dtype),
            pl.BlockSpec((1, rows, STEP), lambda i: (i, 0, 0)),
        )

    outs = [
        strip(3 * width), strip(width), strip(CHAR_HEADS * letters, f32), strip(width), strip(1, f32),
        strip(width), strip(1, f32), strip(hidden), strip(hidden),
        (jax.ShapeDtypeStruct((width, tokens // letters), f32), pl.BlockSpec((width, LANES), lambda i: (0, i // per))),
    ]
    return pl.pallas_call(
        functools.partial(char_forward_kernel, letters),
        grid=(steps,),
        in_specs=[
            pl.BlockSpec((STEP, width), lambda i: (i, 0)),
            pl.BlockSpec((1, 1, STEP), lambda i: (i, 0, 0)),
            pl.BlockSpec((1, LANES), lambda i: (0, i // per)),
        ] + [full_spec(a) for a in (ga, gb, wqkv_t, wproj_t, wup_t, wdown_t)],
        out_specs=[o[1] for o in outs],
        out_shape=[o[0] for o in outs],
        compiler_params=pltpu.CompilerParams(
            dimension_semantics=("arbitrary",), vmem_limit_bytes=56 * 2**20
        ),
        name="char_forward",
    )(x, tok, cnt, ga, gb, wqkv_t, wproj_t, wup_t, wdown_t)


def norm_back(dy, z, rs, gain):
    dz = dy * gain
    a = jnp.mean(dz, 0, keepdims=True)
    b = jnp.mean(dz * z, 0, keepdims=True)
    return rs * (dz - a - z * b)


def fold_lanes(v):
    out = v[:, :LANES]
    for n in range(1, v.shape[1] // LANES):
        out = out + v[:, n * LANES : (n + 1) * LANES]
    return out


def char_backward_kernel(
    letters, dp_ref, tok_ref, ga_ref, gb_ref, wqkv_ref, wproj_ref, wup_ref, wdown_ref,
    t_ref, o_ref, p_ref, z1_ref, rs1_ref, z2_ref, rs2_ref, m_ref, gp_ref,
    cg_ref, gqkv_ref, gproj_ref, gup_ref, gdown_ref, gga_ref, ggb_ref,
    dh2_ref, du_ref, dh1b_ref, do_ref, dt_ref,
):
    step = pl.program_id(0)
    width = cg_ref.shape[1]
    head = width // CHAR_HEADS
    scale = head ** (-0.5)
    steps_per_block = LANES * letters // STEP
    owner = lane_word(letters)
    blocks = own_blocks(letters)

    @pl.when(step == 0)
    def _():
        for ref in (gqkv_ref, gproj_ref, gup_ref, gdown_ref, gga_ref, ggb_ref):
            ref[...] = jnp.zeros_like(ref)

    for part in range(STEP // SPAN):
        at = pl.ds(part * SPAN, SPAN)
        word = lax.broadcasted_iota(jnp.int32, (LANES, SPAN), 0)
        col = lax.broadcasted_iota(jnp.int32, (LANES, SPAN), 1)
        first = (step % steps_per_block) * (STEP // letters) + part * (SPAN // letters)
        mine = (col // letters + first == word) & (col % letters < tok_ref[0, :, at])
        scatter = jnp.where(mine, 1.0, 0.0).astype(bf16)
        dh2 = dot(dp_ref[...], scatter)
        dh2b = dh2.astype(bf16)
        dh2_ref[:, at] = dh2b
        for n in range(wdown_ref.shape[0] // 256):
            rows = pl.ds(n * 256, 256)
            du_ref[rows, at] = (dot(wdown_ref[rows, :], dh2b) * gp_ref[0, rows, at].astype(f32)).astype(bf16)
        dy = dot(wup_ref[...], du_ref[:, at])
        z = z2_ref[0, :, at].astype(f32)
        ggb_ref[...] += fold_lanes(dy * z)
        dh1 = dh2 + norm_back(dy, z, rs2_ref[0, :, at], wide(gb_ref[...], SPAN))
        dh1b = dh1.astype(bf16)
        dh1b_ref[:, at] = dh1b
        do_ref[:, at] = dot(wproj_ref[...], dh1b).astype(bf16)
        for g in range(SPAN // LANES):
            lanes = pl.ds(part * SPAN + g * LANES, LANES)
            for h in range(CHAR_HEADS):
                q_rows = pl.ds(h * head, head)
                k_rows = pl.ds(width + h * head, head)
                v_rows = pl.ds(2 * width + h * head, head)
                q = t_ref[0, q_rows, lanes]
                k = t_ref[0, k_rows, lanes]
                v = t_ref[0, v_rows, lanes]
                do = do_ref[pl.ds(h * head, head), lanes]
                p = p_ref[0, pl.ds(h * letters, letters), lanes]
                dp = pick_own(dot(v.T, do), owner, letters)
                ds = p * (dp - jnp.sum(p * dp, 0, keepdims=True))
                pb = spread_own(p.astype(bf16), blocks, letters)
                dsb = spread_own(ds.astype(bf16), blocks, letters)
                dt_ref[q_rows, lanes] = (dot(k, dsb) * scale).astype(bf16)
                dt_ref[k_rows, lanes] = (dot_nt(q, dsb) * scale).astype(bf16)
                dt_ref[v_rows, lanes] = dot_nt(do, pb).astype(bf16)
        dy = dot(wqkv_ref[...], dt_ref[:, at])
        z = z1_ref[0, :, at].astype(f32)
        gga_ref[...] += fold_lanes(dy * z)
        dx = dh1 + norm_back(dy, z, rs1_ref[0, :, at], wide(ga_ref[...], SPAN))
        cg_ref[at, :] = dx.T.astype(bf16)
    gdown_ref[...] += dot_nt(m_ref[0], dh2_ref[...])
    gup_ref[...] += dot_nt(z2_ref[0], du_ref[...])
    gproj_ref[...] += dot_nt(o_ref[0], dh1b_ref[...])
    gqkv_ref[...] += dot_nt(z1_ref[0], dt_ref[...])

    @pl.when(step == pl.num_programs(0) - 1)
    def _():
        gup_ref[...] = gup_ref[...] * wide(gb_ref[...], gup_ref.shape[1])
        gqkv_ref[...] = gqkv_ref[...] * wide(ga_ref[...], gqkv_ref.shape[1])


def char_backward(dp, tok, ga, gb, wqkv, wproj, wup, wdown, saved, letters):
    t, o, p, z1, rs1, z2, rs2, m, gp = saved
    steps = t.shape[0]
    width = wqkv.shape[0]
    hidden = wup.shape[1]
    per = LANES * letters // STEP

    def whole(shape):
        return (jax.ShapeDtypeStruct(shape, f32), pl.BlockSpec(shape, lambda i: (0, 0)))

    outs = [
        (jax.ShapeDtypeStruct((steps * STEP, width), bf16), pl.BlockSpec((STEP, width), lambda i: (i, 0))),
        whole((width, 3 * width)), whole((width, width)), whole((width, hidden)), whole((hidden, width)),
        whole((width, LANES)), whole((width, LANES)),
    ]
    return pl.pallas_call(
        functools.partial(char_backward_kernel, letters),
        grid=(steps,),
        in_specs=[
            pl.BlockSpec((width, LANES), lambda i: (0, i // per)),
            pl.BlockSpec((1, 1, STEP), lambda i: (i, 0, 0)),
        ] + [full_spec(a) for a in (ga, gb, wqkv, wproj, wup, wdown)]
        + [pl.BlockSpec((1,) + s.shape[1:], lambda i: (i, 0, 0)) for s in saved],
        out_specs=[o[1] for o in outs],
        out_shape=[o[0] for o in outs],
        scratch_shapes=[
            pltpu.VMEM((width, STEP), bf16),
            pltpu.VMEM((hidden, STEP), bf16),
            pltpu.VMEM((width, STEP), bf16),
            pltpu.VMEM((width, STEP), bf16),
            pltpu.VMEM((3 * width, STEP), bf16),
        ],
        compiler_params=pltpu.CompilerParams(
            dimension_semantics=("arbitrary",), vmem_limit_bytes=56 * 2**20
        ),
        name="char_backward",
    )(dp, tok, ga, gb, wqkv, wproj, wup, wdown, *saved)


def word_kernel(
    pool_sum_ref, cnt_ref, sep_ref, cot_ref, ga_ref, gb_ref, wpool_ref, wqkv_ref, wproj_ref, wup_ref, wdown_ref,
    out_ref, dpool_ref, gpool_ref, gqkv_ref, gproj_ref, gup_ref, gdown_ref, gga_ref, ggb_ref,
    pooled, x, z3, rs3, a3, t, p, o, h3, z4, rs4, a4, m, gp, bias, cot, du, dh3, dh3b, do, dt, dtk,
):
    width, length = x.shape
    head = width // WORD_HEADS
    scale = head ** (-0.5)
    halves = [pl.ds(n * SPAN, SPAN) for n in range(length // SPAN)]
    pooled[...] = (pool_sum_ref[...] / cnt_ref[...]).astype(bf16)
    row = lax.broadcasted_iota(jnp.int32, (length, length), 0)
    col = lax.broadcasted_iota(jnp.int32, (length, length), 1)
    tri = jnp.where(row <= col, 1.0, 0.0).astype(bf16)
    sep = jnp.broadcast_to(sep_ref[...].astype(f32).astype(bf16), (16, length))
    doc_q = dot(sep, tri)[:1]
    doc_k = lax.dot_general(tri, sep, (((0,), (1,)), ((), ())), preferred_element_type=f32)[:, :1]
    bias[...] = jnp.where((row <= col) & (doc_k == doc_q), 0.0, NEGATIVE)
    cot[...] = cot_ref[...].astype(f32).T.astype(bf16)
    for at in halves:
        x[:, at] = lax.dot_general(
            wpool_ref[...], pooled[:, at], (((0,), (0,)), ((), ())), preferred_element_type=f32
        )
        z, rs = normed(x[:, at])
        z3[:, at] = z.astype(bf16)
        rs3[:, at] = rs
        a3[:, at] = (z * wide(ga_ref[...], SPAN)).astype(bf16)
        for n in range(3):
            rows = pl.ds(n * width, width)
            t[rows, at] = lax.dot_general(
                wqkv_ref[:, rows], a3[:, at], (((0,), (0,)), ((), ())), preferred_element_type=f32
            ).astype(bf16)
    for h in range(WORD_HEADS):
        k = t[pl.ds(width + h * head, head), :].T
        for n, at in enumerate(halves):
            seen = (n + 1) * SPAN
            keys = pl.ds(0, seen)
            q = t[pl.ds(h * head, head), at]
            s = dot(k[:seen], q) * scale + bias[keys, at]
            e = jnp.exp(s - jnp.max(s, 0, keepdims=True))
            w = e / jnp.sum(e, 0, keepdims=True)
            p[h, keys, at] = w
            o[pl.ds(h * head, head), at] = dot(t[pl.ds(2 * width + h * head, head), keys], w.astype(bf16)).astype(bf16)
    for at in halves:
        h3[:, at] = x[:, at] + lax.dot_general(
            wproj_ref[...], o[:, at], (((0,), (0,)), ((), ())), preferred_element_type=f32
        )
        z, rs = normed(h3[:, at])
        z4[:, at] = z.astype(bf16)
        rs4[:, at] = rs
        a4[:, at] = (z * wide(gb_ref[...], SPAN)).astype(bf16)
        for n in range(wup_ref.shape[1] // 256):
            rows = pl.ds(n * 256, 256)
            mm, gg = gelu_both(
                lax.dot_general(wup_ref[:, rows], a4[:, at], (((0,), (0,)), ((), ())), preferred_element_type=f32)
            )
            m[rows, at] = mm.astype(bf16)
            gp[rows, at] = gg.astype(bf16)
        out = h3[:, at] + lax.dot_general(
            wdown_ref[...], m[:, at], (((0,), (0,)), ((), ())), preferred_element_type=f32
        )
        out_ref[at, :] = out.T.astype(bf16)
        for n in range(wdown_ref.shape[0] // 256):
            rows = pl.ds(n * 256, 256)
            du[rows, at] = (dot(wdown_ref[rows, :], cot[:, at]) * gp[rows, at].astype(f32)).astype(bf16)
        dy = dot(wup_ref[...], du[:, at])
        z = z4[:, at].astype(f32)
        part = fold_lanes(dy * z)
        ggb_ref[...] = part if at is halves[0] else ggb_ref[...] + part
        dh3[:, at] = cot[:, at].astype(f32) + norm_back(dy, z, rs4[:, at], wide(gb_ref[...], SPAN))
        dh3b[:, at] = dh3[:, at].astype(bf16)
        do[:, at] = dot(wproj_ref[...], dh3b[:, at]).astype(bf16)
    gdown_ref[...] = dot_nt(m[...], cot[...]).astype(gdown_ref.dtype)
    gup_ref[...] = dot_nt(a4[...], du[...]).astype(gup_ref.dtype)
    gproj_ref[...] = dot_nt(o[...], dh3b[...]).astype(gproj_ref.dtype)
    for h in range(WORD_HEADS):
        q_rows = pl.ds(h * head, head)
        k_rows = pl.ds(width + h * head, head)
        v_rows = pl.ds(2 * width + h * head, head)
        v = t[v_rows, :].T
        for n in reversed(range(len(halves))):
            at = halves[n]
            seen = (n + 1) * SPAN
            keys = pl.ds(0, seen)
            w = p[h, keys, at]
            g = do[q_rows, at]
            dp = dot(v[:seen], g)
            ds = (w * (dp - jnp.sum(w * dp, 0, keepdims=True))).astype(bf16)
            dt[q_rows, at] = (dot(t[k_rows, keys], ds) * scale).astype(bf16)
            dk = dot_nt(t[q_rows, at], ds) * scale
            dv = dot_nt(g, w.astype(bf16))
            if n == len(halves) - 1:
                dtk[0] = dk
                dtk[1] = dv
            else:
                dtk[0, :, keys] += dk
                dtk[1, :, keys] += dv
        dt[k_rows, :] = dtk[0].astype(bf16)
        dt[v_rows, :] = dtk[1].astype(bf16)
    gqkv_ref[...] = dot_nt(a3[...], dt[...]).astype(gqkv_ref.dtype)
    for at in halves:
        dy = dot(wqkv_ref[...], dt[:, at])
        z = z3[:, at].astype(f32)
        part = fold_lanes(dy * z)
        gga_ref[...] = part if at is halves[0] else gga_ref[...] + part
        dx = dh3[:, at] + norm_back(dy, z, rs3[:, at], wide(ga_ref[...], SPAN))
        dh3b[:, at] = dx.astype(bf16)
        dpool_ref[:, at] = (dot(wpool_ref[...], dh3b[:, at]) / cnt_ref[:, at]).astype(bf16)
    gpool_ref[...] = dot_nt(pooled[...], dh3b[...]).astype(gpool_ref.dtype)


def word_layer(pool_sum, cnt, sep, cot, ga, gb, wpool, wqkv, wproj, wup, wdown, grad_type=f32):
    length, width = cot.shape
    inner = pool_sum.shape[0]
    hidden = wup.shape[1]
    vm = pltpu.VMEM
    return pl.pallas_call(
        word_kernel,
        out_shape=[
            jax.ShapeDtypeStruct((length, width), bf16),
            jax.ShapeDtypeStruct((inner, length), bf16),
            jax.ShapeDtypeStruct(wpool.shape, grad_type),
            jax.ShapeDtypeStruct(wqkv.shape, grad_type),
            jax.ShapeDtypeStruct(wproj.shape, grad_type),
            jax.ShapeDtypeStruct(wup.shape, grad_type),
            jax.ShapeDtypeStruct(wdown.shape, grad_type),
            jax.ShapeDtypeStruct((width, LANES), f32),
            jax.ShapeDtypeStruct((width, LANES), f32),
        ],
        scratch_shapes=[
            vm((inner, length), bf16), vm((width, length), f32), vm((width, length), bf16), vm((1, length), f32),
            vm((width, length), bf16), vm((3 * width, length), bf16), vm((WORD_HEADS, length, length), f32),
            vm((width, length), bf16), vm((width, length), f32), vm((width, length), bf16), vm((1, length), f32),
            vm((width, length), bf16), vm((hidden, length), bf16), vm((hidden, length), bf16),
            vm((length, length), f32), vm((width, length), bf16), vm((hidden, length), bf16),
            vm((width, length), f32), vm((width, length), bf16), vm((width, length), bf16),
            vm((3 * width, length), bf16), vm((2, width // WORD_HEADS, length), f32),
        ],
        compiler_params=pltpu.CompilerParams(vmem_limit_bytes=58 * 2**20),
        name="word_layer",
    )(pool_sum, cnt, sep, cot, ga, gb, wpool, wqkv, wproj, wup, wdown)


def gather_all(shards, counts):
    flat = jnp.concatenate([s.reshape(-1) for s in shards])
    packed = lax.all_gather(lax.all_gather(flat, "fsdp", axis=0), "dp", axis=0)
    wide_count, deep_count = packed.shape[:2]
    out, start = [], 0
    for s in shards:
        piece = packed[:, :, start : start + s.size]
        start += s.size
        if s.ndim == 1:
            out.append(piece[:, 0].reshape(-1))
        else:
            r, c = s.shape
            piece = piece.reshape(wide_count, deep_count, r, c).transpose(1, 2, 0, 3)
            out.append(piece.reshape(deep_count * r, wide_count * c))
    return out


def scatter_all(grads, shards):
    wide_count, deep_count = lax.axis_size("dp"), lax.axis_size("fsdp")
    pieces = []
    for g, s in zip(grads, shards):
        g = g.astype(bf16)
        if s.ndim == 1:
            g = jnp.broadcast_to(g.reshape(wide_count, 1, s.size), (wide_count, deep_count, s.size))
        else:
            r, c = s.shape
            g = g.reshape(deep_count, r, wide_count, c).transpose(2, 0, 1, 3)
        pieces.append(g.reshape(wide_count, deep_count, s.size))
    packed = jnp.concatenate(pieces, 2)
    packed = lax.psum_scatter(packed, "dp", scatter_dimension=0, tiled=True)
    packed = lax.psum_scatter(packed, "fsdp", scatter_dimension=1, tiled=True).reshape(-1)
    out, start = [], 0
    for s in shards:
        out.append(packed[start : start + s.size].reshape(s.shape).astype(f32))
        start += s.size
    return out


def shards(
    characters, counts, separators, cotangent, char_qkv, char_proj, char_up, char_down, char_gain_a, char_gain_b,
    pool_proj, word_qkv, word_proj, word_up, word_down, word_gain_a, word_gain_b,
):
    rows, length, letters, width = characters.shape
    char_shards = (char_qkv, char_proj, char_up, char_down, char_gain_a, char_gain_b)
    word_shards = (pool_proj, word_qkv, word_proj, word_up, word_down, word_gain_a, word_gain_b)
    cqkv, cproj, cup, cdown, cga, cgb = gather_all(char_shards, counts)
    wpool, wqkv, wproj, wup, wdown, wga, wgb = gather_all(word_shards, counts)
    x = characters.reshape(length * letters, width)
    tok = jnp.repeat(counts, letters, axis=1).reshape(length * letters // STEP, 1, STEP)
    cga, cgb, wga, wgb = (
        jnp.broadcast_to(g.astype(f32)[:, None], (g.shape[0], LANES)) for g in (cga, cgb, wga, wgb)
    )
    *saved, pool_sum = char_forward(x, tok, counts, cga, cgb, cqkv.T, cproj.T, cup.T, cdown.T, letters)
    word_out, dpool, gpool, gwqkv, gwproj, gwup, gwdown, gwga, gwgb = word_layer(
        pool_sum, counts.astype(f32), separators, cotangent.reshape(length, -1), wga, wgb, wpool, wqkv, wproj, wup, wdown
    )
    word_grads = scatter_all(
        (gpool, gwqkv, gwproj, gwup, gwdown, jnp.sum(gwga, 1), jnp.sum(gwgb, 1)), word_shards
    )
    char_grad, gcqkv, gcproj, gcup, gcdown, gcga, gcgb = char_backward(
        dpool, tok, cga, cgb, cqkv, cproj, cup, cdown, saved, letters
    )
    char_grads = scatter_all(
        (gcqkv, gcproj, gcup, gcdown, jnp.sum(gcga, 1), jnp.sum(gcgb, 1)), char_shards
    )
    return (word_out[None], char_grad.reshape(characters.shape), *char_grads, *word_grads)


def solution(mesh):
    rows = ("dp", "fsdp")
    matrix, vector = P("fsdp", "dp"), P("dp")
    data = (P(rows, None, None, None), P(rows, None), P(rows, None), P(rows, None, None))
    block = (matrix,) * 4 + (vector,) * 2
    word = (matrix,) * 5 + (vector,) * 2
    return jax.shard_map(
        shards,
        mesh=mesh,
        in_specs=data + block + word,
        out_specs=(data[3], data[0]) + block + word,
        check_vma=False,
    )
```

time: 1220 us -> 709 us (0.58)
  matrix products: 292 us -> 0 us
  Pallas kernels: 0 us -> 222 us
  blocking collectives: 216 us -> 28.9 us
  waiting for transfers between devices: 407 us -> 247 us
  other arithmetic: 96.5 us -> 28.3 us
  local copies, waits for them, and re-layouts: 177 us -> 159 us
    dot_general x39 -> x0, matrix products: 292 us -> none  [the longest x9 74.6 us: contract_cols(): lax.dot_general(left_op, right_op, (((1,), (1,)), ((), ())), preferred_el...]
    pallas_call x0 -> x3, Pallas kernels: none -> 222 us  [the longest x1 109 us: char_backward(): pl.pallas_call(functools.partial(char_backward_kernel, letters), grid=(st...]
    reduce_scatter x10 -> x0, waiting for transfers between devices: 164 us -> none  [the longest x1 35.5 us: shards(): lax.psum_scatter(row_parts[7].astype(jnp.bfloat16), 'dp', scatter_dimensi...]
    all_gather x15 -> x1, blocking collectives: 181 us -> 28.9 us  [gather_all(): packed = lax.all_gather(lax.all_gather(flat, 'fsdp', axis=0), 'dp', axis=0)]
    unnamed x233 -> x70, local copies, waits for them, and re-layouts: 80.3 us -> 34.1 us
    reduce_sum x11 -> x4, other arithmetic: 38.8 us -> 2.33 us  [the longest x1 1.02 us: shards(): jnp.sum(gcgb, 1)]
    convert_element_type x23 -> x20, other arithmetic: 53.4 us -> 25.8 us  [the longest x9 16.7 us: scatter_all(): out.append(packed[start:start + s.size].reshape(s.shape).astype(f32))]
    unnamed x2 -> x0, blocking collectives: 25 us -> none
  transfers between devices with their start and end apart: 21 -> 5, of which waited for: 13 -> 3; matrix products, arithmetic and copies ran while one was open for 31% -> 4% of each run, Pallas kernels for 0% -> 11%
where the time goes in v1:
time: 709 us; the launch traced here: 701 us
  waiting for transfers between devices  247 us (35%)
  Pallas kernels  222 us (31%)
  local copies, waits for them, and re-layouts  159 us (22%)
  blocking collectives  28.9 us (4%)
  other arithmetic  28.3 us (4%)
  between operations  15.8 us (2%)
    unnamed x8, waiting for transfers between devices  247 us
    pallas_call x1, Pallas kernels, char_backward(): pl.pallas_call(functools.partial(char_backward_kernel, letters), grid=(st...  109 us
    pallas_call x1, Pallas kernels, char_forward(): pl.pallas_call(functools.partial(char_forward_kernel, letters), grid=(ste...  80.3 us
    unnamed x70, local copies, waits for them, and re-layouts  34.1 us
    pallas_call x1, Pallas kernels, word_layer(): pl.pallas_call(word_kernel, out_shape=[jax.ShapeDtypeStruct((length, widt...  31.9 us
    all_gather x1, blocking collectives, gather_all(): packed = lax.all_gather(lax.all_gather(flat, 'fsdp', axis=0), 'dp', axis=0)  28.9 us
    reshape x11, local copies, waits for them, and re-layouts, gather_all(): out.append(piece.reshape(deep_count * r, wide_count * c))  26.3 us
    reshape x9, local copies, waits for them, and re-layouts, gather_all(): piece = piece.reshape(wide_count, deep_count, r, c).transpose(1, 2, 0, 3)  17.2 us
  transfers between devices with their start and end apart: 5, of which 3 were waited for; matrix products, arithmetic and copies ran while one was open for 4% of the time, Pallas kernels for 11%

profile of v1, /device:TPU:0, one launch (start us, length us, event | category | flops | bytes accessed | tf_op | source)
XLA Modules:
  0.0 701.0 jit_solution(4761028243134877310)
XLA Ops:
  12.0 2.1 concatenate.12
  15.5 37.4 %all-reduce.11.cloned.1.call-done = bf16[98560]{0:T(1024)(128)(2,1)} async-done(((bf16[98560]{0:T(1024)(128)(2,1)}), bf16[98560]{0:T(1024)(128)(2,1)}) %all-reduce.11.cloned.1.call-update) | async-done | bytes 197136
  60.5 28.9 %all-gather.5 = bf16[4,1,102528]{2,1,0:T(2,128)(2,1)S(1)} all-gather(bf16[1,1,102528]{2,1,0:T(2,128)(2,1)S(1)} %reshape.373), channel_id=4, replica_groups=mesh['dp'=8,'fsdp'=4] {'fsdp'}, dimensions={0}, use_global_device_ids=true | all-gather | bytes 1025280 | tf_op jit(solution)/shard_map/all_gather | solution.py:444
  109.2 80.3 %char_forward.1 = (bf16[16,768,512]{2,1,0:T(8,128)(2,1)}, bf16[16,256,512]{2,1,0:T(8,128)(2,1)}, f32[16,64,512]{2,1,0:T(8,128)}, bf16[16,256,512]{2,1,0:T(8,128)...) custom-call(bf16[8192,256]{1,0:T(8,128)(2,1)} %bitcast.168, ...), custom_call_target="tpu_custom_call" | custom-call | tf_op jit(solution)/shard_map/char_forward/pallas_call | solution.py:157
  196.2 3.5 reshape.320
  199.8 2.5 copy.194
  202.3 4.6 reshape.389.wqkv_ref
  210.4 4.4 fusion.21
  214.8 3.2 reshape.391
  219.2 2.1 copy.206
  222.5 5.5 reshape.326
  228.1 6.8 copy.198
  234.9 6.8 reshape.392.wdown_ref
  243.4 31.9 %word_layer.1 = (bf16[512,512]{1,0:T(8,128)(2,1)}, bf16[256,512]{1,0:T(8,128)(2,1)}, f32[256,512]{1,0:T(8,128)}, f32[512,1536]{1,0:T(8,128)}, f32[512,512]{1,0:T...) custom-call(f32[256,512]{1,0:T(8,128)} %get-tuple-element.41.pool_sum_ref, ...), custom_call_target="tpu_custom_call" | custom-call | tf_op jit(solution)/shard_map/word_layer/pallas_call | solution.py:415
  275.3 109.4 %char_backward.1 = (bf16[8192,256]{1,0:T(8,128)(2,1)}, f32[256,768]{1,0:T(8,128)}, f32[256,256]{1,0:T(8,128)}, f32[256,1024]{1,0:T(8,128)}, f32[1024,256]{1,0:T(...) custom-call(bf16[256,512]{1,0:T(8,128)(2,1)} %get-tuple-element.43.dp_ref, s32[16,1,512]{2,1,0:T(1,128)} %broadcast_in_dim.66.tok_ref, ...), custom_call_target="tpu_custom_call" | custom-call | tf_op jit(solution)/shard_map/char_backward/pallas_call | solution.py:276
  391.1 2.3 reshape.336
  400.9 2.1 convert_element_type.218
  405.5 2.8 copy.180
  408.3 3.5 reshape.340
  413.8 2.5 convert_element_type.220
  419.5 2.4 copy.183
  421.9 3.3 reshape.345
  425.3 4.3 copy.184
  429.6 5.0 reshape.346
  435.1 2.8 constant_dynamic-update-slice_fusion.3
  444.6 8.1 %copy.185 = bf16[8,4,102528]{2,1,0:T(4,128)(2,1)} copy(bf16[8,4,102528]{2,0,1:T(8,128)(2,1)} %dynamic-update-slice.7) | data formatting | bytes 13123584 | tf_op jit(solution)/shard_map/concatenate | solution.py:470
  454.0 124.6 %all-reduce.13.cloned.1.call-done = (bf16[8,4,24640]{2,1,0:T(4,128)(2,1)}, bf16[8,4,102528]{2,1,0:T(4,128)(2,1)}) async-done(((bf16[8,4,24640]{2,1,0:T(4,128)(2,1)}, bf16[8,4,102528]{2,1,0:T(4,128)(2,1)}), (bf16[8,4,24640]{2,1,0:T(4,128)(2,1)}, bf16[8,4,102528]{2,1,0:T(4,128)(2,1)})) %all-reduce.13.cloned.1.call-update) | async-done | bytes 8138768
  581.3 2.1 constant_dynamic-slice_fusion.3
  583.4 2.4 copy.186
  585.8 85.3 %all-reduce.15.cloned.1.call-done = (bf16[1,4,24640]{2,0,1:T(2,128)(2,1)}, bf16[1,4,102528]{2,0,1:T(2,128)(2,1)}) async-done(((bf16[1,4,24640]{2,0,1:T(2,128)(2,1)}, bf16[1,4,102528]{2,0,1:T(2,128)(2,1)}), (bf16[1,4,24640]{2,0,1:T(2,128)(2,1)}, bf16[1,4,102528]{2,0,1:T(2,128)(2,1)})) %all-reduce.15.cloned.1.call-update) | async-done | bytes 1017360
  675.5 2.2 dynamic-slice_convert_fusion.5
  685.9 2.4 fusion
  (196 shorter events, 97.5 us)
Async XLA Ops:
  7.2 52.5 %copy-start.16 = (bf16[64]{0:T(256)(128)(2,1)S(1)}, bf16[64]{0:T(256)(128)(2,1)}, u32[]{:S(2)}) copy-start(bf16[64]{0:T(256)(128)(2,1)} %param.32) | copy-start | bytes 388
  7.2 52.5 %copy-start.17 = (bf16[64]{0:T(256)(128)(2,1)S(1)}, bf16[64]{0:T(256)(128)(2,1)}, u32[]{:S(2)}) copy-start(bf16[64]{0:T(256)(128)(2,1)} %param.33) | copy-start | bytes 388
  7.2 45.7 %all-reduce.11.cloned.1.call-start = ((), (), s32[]{:S(2)}) async-start(), calls=%async_computation | async-start | bytes 397312
  14.8 0.7 copy-start.10
  15.5 78.0 %all-gather.10.cloned.1.call-start = ((), (), s32[]{:S(2)}) async-start(), calls=%async_computation.1 | async-start | bytes 1778688 | tf_op jit(solution)/shard_map/all_gather | solution.py:444
  54.9 134.7 %all-gather.12.cloned.1.call-start = ((), (), s32[]{:S(2)}) async-start(), calls=%async_computation.2 | async-start | bytes 7382016 | tf_op jit(solution)/shard_map/all_gather | solution.py:444
  89.3 1.9 copy-start.15
  90.7 487.9 %all-reduce.13.cloned.1.call-start = ((), (), s32[]{:S(2)}) async-start(), calls=%async_computation.3 | async-start | bytes 16285696
  95.8 2.3 slice-start.2
  97.2 3.6 copy-start.5
  99.0 6.8 copy-start.6
  101.7 3.1 copy-start.2
  105.9 3.3 copy-start.3
  192.7 1.5 slice-start
  202.3 4.6 slice-start.1
  219.2 2.2 copy-start.1
  384.7 2.7 copy-start.12
  386.5 2.7 copy-start.9
  388.0 1.4 copy-start.8
  397.5 1.8 copy-start.11
  408.3 3.5 copy-start.7
  416.3 2.9 copy-start.4
  429.6 5.0 copy-start.14
  429.6 5.3 copy-start.13
  435.1 3.7 copy-start
  452.7 0.7 copy-start.18
  452.8 218.4 %all-reduce.15.cloned.1.call-start = ((), (), s32[]{:S(2)}) async-start(), calls=%async_computation.4 | async-start | bytes 4071424
Sparse Core Ops, SparseCore 0:
  15.6 37.2 all-reduce.10
  55.5 25.7 all-gather.9
  90.8 47.2 all-gather.11
  452.9 125.6 all-reduce.12
  585.9 85.1 all-reduce.14

commit v2 on v1

--- a/solution.py
+++ b/solution.py
@@ -1,4 +1,5 @@
 import functools
+import math
 
 import jax
 import jax.numpy as jnp
@@ -295,6 +296,145 @@
         ),
         name="char_backward",
     )(dp, tok, ga, gb, wqkv, wproj, wup, wdown, *saved)
+
+
+def word_gathered_kernel(
+    pool_sum_ref, cnt_ref, sep_ref, cot_ref, ga_ref, gb_ref, wpool_t, all_ref,
+    out_ref, dpool_ref, gpool_ref, gqkv_ref, gproj_ref, gup_ref, gdown_ref, gga_ref, ggb_ref,
+    pooled, x, z3, rs3, a3, t, p, o, h3, z4, rs4, a4, m, gp, bias, cot, du, dh3, dh3b, do, dt, dtk,
+    wqkv_t, wproj_t, wup_t, wdown_t, wqkv_ref, wproj_ref, wup_ref, wdown_ref, wpool_ref,
+):
+    unpack_word(all_ref, wqkv_t, wproj_t, wup_t, wdown_t, wqkv_ref, wproj_ref, wup_ref, wdown_ref)
+    wpool_ref[...] = turned(wpool_t[...])
+    width, length = x.shape
+    head = width // WORD_HEADS
+    scale = head ** (-0.5)
+    halves = [pl.ds(n * SPAN, SPAN) for n in range(length // SPAN)]
+    pooled[...] = (pool_sum_ref[...] / cnt_ref[...]).astype(bf16)
+    row = lax.broadcasted_iota(jnp.int32, (length, length), 0)
+    col = lax.broadcasted_iota(jnp.int32, (length, length), 1)
+    tri = jnp.where(row <= col, 1.0, 0.0).astype(bf16)
+    sep = jnp.broadcast_to(sep_ref[...].astype(f32).astype(bf16), (16, length))
+    doc_q = dot(sep, tri)[:1]
+    doc_k = lax.dot_general(tri, sep, (((0,), (1,)), ((), ())), preferred_element_type=f32)[:, :1]
+    bias[...] = jnp.where((row <= col) & (doc_k == doc_q), 0.0, NEGATIVE)
+    cot[...] = cot_ref[...].astype(f32).T.astype(bf16)
+    for at in halves:
+        x[:, at] = dot(wpool_t[...], pooled[:, at])
+        z, rs = normed(x[:, at])
+        z3[:, at] = z.astype(bf16)
+        rs3[:, at] = rs
+        a3[:, at] = (z * wide(ga_ref[...], SPAN)).astype(bf16)
+        for n in range(3):
+            rows = pl.ds(n * width, width)
+            t[rows, at] = dot(wqkv_t[rows, :], a3[:, at]).astype(bf16)
+    for h in range(WORD_HEADS):
+        k = t[pl.ds(width + h * head, head), :].T
+        for n, at in enumerate(halves):
+            seen = (n + 1) * SPAN
+            keys = pl.ds(0, seen)
+            q = t[pl.ds(h * head, head), at]
+            s = dot(k[:seen], q) * scale + bias[keys, at]
+            e = jnp.exp(s - jnp.max(s, 0, keepdims=True))
+            w = e / jnp.sum(e, 0, keepdims=True)
+            p[h, keys, at] = w
+            o[pl.ds(h * head, head), at] = dot(t[pl.ds(2 * width + h * head, head), keys], w.astype(bf16)).astype(bf16)
+    for at in halves:
+        h3[:, at] = x[:, at] + dot(wproj_t[...], o[:, at])
+        z, rs = normed(h3[:, at])
+        z4[:, at] = z.astype(bf16)
+        rs4[:, at] = rs
+        a4[:, at] = (z * wide(gb_ref[...], SPAN)).astype(bf16)
+        for n in range(wup_ref.shape[1] // 256):
+            rows = pl.ds(n * 256, 256)
+            mm, gg = gelu_both(dot(wup_t[rows, :], a4[:, at]))
+            m[rows, at] = mm.astype(bf16)
+            gp[rows, at] = gg.astype(bf16)
+        out = h3[:, at] + dot(wdown_t[...], m[:, at])
+        out_ref[at, :] = out.T.astype(bf16)
+        for n in range(wdown_ref.shape[0] // 256):
+            rows = pl.ds(n * 256, 256)
+            du[rows, at] = (dot(wdown_ref[rows, :], cot[:, at]) * gp[rows, at].astype(f32)).astype(bf16)
+        dy = dot(wup_ref[...], du[:, at])
+        z = z4[:, at].astype(f32)
+        part = fold_lanes(dy * z)
+        ggb_ref[...] = part if at is halves[0] else ggb_ref[...] + part
+        dh3[:, at] = cot[:, at].astype(f32) + norm_back(dy, z, rs4[:, at], wide(gb_ref[...], SPAN))
+        dh3b[:, at] = dh3[:, at].astype(bf16)
+        do[:, at] = dot(wproj_ref[...], dh3b[:, at]).astype(bf16)
+    gdown_ref[...] = dot_nt(m[...], cot[...]).astype(gdown_ref.dtype)
+    gup_ref[...] = dot_nt(a4[...], du[...]).astype(gup_ref.dtype)
+    gproj_ref[...] = dot_nt(o[...], dh3b[...]).astype(gproj_ref.dtype)
+    for h in range(WORD_HEADS):
+        q_rows = pl.ds(h * head, head)
+        k_rows = pl.ds(width + h * head, head)
+        v_rows = pl.ds(2 * width + h * head, head)
+        v = t[v_rows, :].T
+        for n in reversed(range(len(halves))):
+            at = halves[n]
+            seen = (n + 1) * SPAN
+            keys = pl.ds(0, seen)
+            w = p[h, keys, at]
+            g = do[q_rows, at]
+            dp = dot(v[:seen], g)
+            ds = (w * (dp - jnp.sum(w * dp, 0, keepdims=True))).astype(bf16)
+            dt[q_rows, at] = (dot(t[k_rows, keys], ds) * scale).astype(bf16)
+            dk = dot_nt(t[q_rows, at], ds) * scale
+            dv = dot_nt(g, w.astype(bf16))
+            if n == len(halves) - 1:
+                dtk[0] = dk
+                dtk[1] = dv
+            else:
+                dtk[0, :, keys] += dk
+                dtk[1, :, keys] += dv
+        dt[k_rows, :] = dtk[0].astype(bf16)
+        dt[v_rows, :] = dtk[1].astype(bf16)
+    gqkv_ref[...] = dot_nt(a3[...], dt[...]).astype(gqkv_ref.dtype)
+    for at in halves:
+        dy = dot(wqkv_ref[...], dt[:, at])
+        z = z3[:, at].astype(f32)
+        part = fold_lanes(dy * z)
+        gga_ref[...] = part if at is halves[0] else gga_ref[...] + part
+        dx = dh3[:, at] + norm_back(dy, z, rs3[:, at], wide(ga_ref[...], SPAN))
+        dh3b[:, at] = dx.astype(bf16)
+        dpool_ref[:, at] = (dot(wpool_ref[...], dh3b[:, at]) / cnt_ref[:, at]).astype(bf16)
+    gpool_ref[...] = dot_nt(pooled[...], dh3b[...]).astype(gpool_ref.dtype)
+
+
+def word_gathered(pool_sum, cnt, sep, cot, ga, gb, pool_t, gathered, grad_type=f32):
+    length, width = cot.shape
+    inner = pool_sum.shape[0]
+    nd, nz, rows, lanes = gathered.shape
+    hidden = nd * lanes
+    vm = pltpu.VMEM
+    return pl.pallas_call(
+        word_gathered_kernel,
+        out_shape=[
+            jax.ShapeDtypeStruct((length, width), bf16),
+            jax.ShapeDtypeStruct((inner, length), bf16),
+            jax.ShapeDtypeStruct((inner, width), grad_type),
+            jax.ShapeDtypeStruct((width, 3 * width), grad_type),
+            jax.ShapeDtypeStruct((width, width), grad_type),
+            jax.ShapeDtypeStruct((width, hidden), grad_type),
+            jax.ShapeDtypeStruct((hidden, width), grad_type),
+            jax.ShapeDtypeStruct((width, LANES), f32),
+            jax.ShapeDtypeStruct((width, LANES), f32),
+        ],
+        scratch_shapes=[
+            vm((inner, length), bf16), vm((width, length), f32), vm((width, length), bf16), vm((1, length), f32),
+            vm((width, length), bf16), vm((3 * width, length), bf16), vm((WORD_HEADS, length, length), f32),
+            vm((width, length), bf16), vm((width, length), f32), vm((width, length), bf16), vm((1, length), f32),
+            vm((width, length), bf16), vm((hidden, length), bf16), vm((hidden, length), bf16),
+            vm((length, length), f32), vm((width, length), bf16), vm((hidden, length), bf16),
+            vm((width, length), f32), vm((width, length), bf16), vm((width, length), bf16),
+            vm((3 * width, length), bf16), vm((2, width // WORD_HEADS, length), f32),
+            vm((3 * width, width), bf16), vm((width, width), bf16), vm((hidden, width), bf16), vm((width, hidden), bf16),
+            vm((width, 3 * width), bf16), vm((width, width), bf16), vm((width, hidden), bf16), vm((hidden, width), bf16),
+            vm((inner, width), bf16),
+        ],
+        compiler_params=pltpu.CompilerParams(vmem_limit_bytes=58 * 2**20),
+        name="word_gathered",
+    )(pool_sum, cnt, sep, cot, ga, gb, pool_t, gathered)
 
 
 def word_kernel(
@@ -439,6 +579,293 @@
     )(pool_sum, cnt, sep, cot, ga, gb, wpool, wqkv, wproj, wup, wdown)
 
 
+MESH = pl.DeviceIdType.MESH
+
+
+def sides():
+    chips = lax.axis_size("dp") // 2
+    nx = math.isqrt(chips)
+    return chips // nx, nx, lax.axis_size("fsdp")
+
+
+def place():
+    ny, nx, nz = sides()
+    me = lax.axis_index("dp")
+    return me // (2 * nx), (me // 2) % nx, me % 2, lax.axis_index("fsdp")
+
+
+def device(y, x, c, z):
+    return {"dp": (y * sides()[1] + x) * 2 + c, "fsdp": z}
+
+
+def partners():
+    ny, nx, nz = sides()
+    y, x, c, z = place()
+    found = [device(y, x, 1 - c, z)]
+    found += [device(y, x, c, (z + k) % nz) for k in range(1, nz)]
+    found += [device(y, (x + k) % nx, c, z) for k in range(1, nx)]
+    found += [device((y + k) % ny, x, c, z) for k in range(1, ny)]
+    return found
+
+
+def greet():
+    barrier = pltpu.get_barrier_semaphore()
+    for other in partners():
+        pl.semaphore_signal(barrier, inc=1, device_id=other, device_id_type=MESH)
+    pl.semaphore_wait(barrier, len(partners()))
+
+
+def gather_copies():
+    ny, nx, nz = sides()
+    return nz - 1 + 1 + 4 * (nx - 1) + 4 * (ny - 1)
+
+
+def gather_stages(ref, sems):
+    ny, nx, nz = sides()
+    y, x, c, z = place()
+    every = slice(None)
+    half = ref.shape[4] // 2
+    low, high = pl.ds(0, half), pl.ds(half, half)
+    twin = device(y, x, 1 - c, z)
+    plan = [[], [], [], []]
+    plan[0] += [((y, x, c, z), device(y, x, c, (z + k) % nz)) for k in range(1, nz)]
+    plan[1] += [((y, x, c, every, low), device(y, (x + k) % nx, c, z)) for k in range(1, nx)]
+    plan[1] += [((y, x, c, every, high), device((y + k) % ny, x, c, z)) for k in range(1, ny)]
+    plan[1] += [((y, x, c), twin)]
+    plan[2] += [((y, every, c, every, low), device((y + k) % ny, x, c, z)) for k in range(1, ny)]
+    plan[2] += [((every, x, c, every, high), device(y, (x + k) % nx, c, z)) for k in range(1, nx)]
+    plan[2] += [((y, (x + k) % nx, c, every, low), twin) for k in range(1, nx)]
+    plan[2] += [(((y + k) % ny, x, c, every, high), twin) for k in range(1, ny)]
+    plan[3] += [(((y + k) % ny, every, c, every, low), twin) for k in range(1, ny)]
+    plan[3] += [((every, (x + k) % nx, c, every, high), twin) for k in range(1, nx)]
+    count = 0
+    stages = []
+    for part in plan:
+        copies = []
+        for where, other in part:
+            copies.append(
+                pltpu.make_async_remote_copy(
+                    src_ref=ref.at[where], dst_ref=ref.at[where], send_sem=sems.at[0, count],
+                    recv_sem=sems.at[1, count], device_id=other, device_id_type=MESH,
+                )
+            )
+            count += 1
+        stages.append(copies)
+    return stages
+
+
+def start_all(copies):
+    for copy in copies:
+        copy.start()
+
+
+def arrive_all(copies):
+    for copy in copies:
+        copy.wait_recv()
+
+
+def sent_all(stages):
+    for copies in stages:
+        for copy in copies:
+            copy.wait_send()
+
+
+def lanes_to(v, n):
+    return v if v.shape[1] == n else jnp.concatenate([v, jnp.zeros((v.shape[0], n - v.shape[1]), v.dtype)], 1)
+
+
+def turned(v):
+    return v.astype(f32).T.astype(bf16)
+
+
+def pack_char(slot, qkv, proj, up, down, pool, gains):
+    r = up.shape[0]
+    slot[pl.ds(0, r), :] = jnp.concatenate([qkv[...], proj[...]], 1)
+    slot[pl.ds(r, r), :] = up[...]
+    down_t = turned(lanes_to(down[...], LANES))[: down.shape[1]]
+    slot[pl.ds(2 * r, r // 2), :] = down_t[:, :LANES]
+    slot[pl.ds(2 * r + r // 2, r // 2), :] = down_t[:, LANES:]
+    side = jnp.concatenate([gains[...], jnp.zeros((r - gains.shape[0], gains.shape[1]), f32)], 0).astype(bf16)
+    slot[pl.ds(3 * r, r), :] = jnp.concatenate([pool[...], side], 1)
+
+
+def pack_word(slot, qkv, proj, up, down):
+    r = up.shape[0]
+    slot[pl.ds(0, r), :] = jnp.concatenate([qkv[...], proj[...]], 1)
+    slot[pl.ds(r, r), :] = up[...]
+    down_t = turned(lanes_to(down[...], LANES))[: down.shape[1]]
+    n = down_t.shape[1] // 2
+    slot[pl.ds(2 * r, r // 2), :] = down_t[:, :n]
+    slot[pl.ds(2 * r + r // 2, r // 2), :] = down_t[:, n:]
+
+
+def unpack_char(all_ref, wqkv_t, wproj_t, wup_t, wdown_t, wqkv, wproj, wup, wdown, pool_t, cga, cgb, wga, wgb):
+    ny, nx, nz = sides()
+    r = all_ref.shape[4] // 4
+    width = nz * r
+    nd = ny * nx * 2
+    a, b = wqkv_t.shape[0] // nd, wproj_t.shape[0] // nd
+    n = wdown_t.shape[0] // nd
+    deep = wdown_t.shape[1] // nz
+    p = pool_t.shape[0] // nd
+    gc = cga.shape[0] // nd
+    for d in range(nd):
+        at = (d // (2 * nx), (d // 2) % nx, d % 2)
+
+        def column(row, rows):
+            return all_ref[at + (slice(None), pl.ds(row, rows), slice(None))].reshape(nz * rows, LANES)
+
+        t = turned(column(0, r))
+        wqkv_t[pl.ds(d * a, a), :] = t[:a]
+        wproj_t[pl.ds(d * b, b), :] = t[a:]
+        up = column(r, r)
+        wup[:, pl.ds(d * LANES, LANES)] = up
+        wup_t[pl.ds(d * LANES, LANES), :] = turned(up)
+        for z in range(nz):
+            for s in range(2):
+                wdown_t[pl.ds(d * n, n), pl.ds(z * deep + s * LANES, LANES)] = all_ref[
+                    at + (z, pl.ds(2 * r + s * n, n), slice(None))
+                ]
+        t = column(3 * r, r).astype(f32).T
+        pool_t[pl.ds(d * p, p), :] = t[:p].astype(bf16)
+        one, two, three = (jnp.broadcast_to(t[p:, i : i + 1], (p, LANES)) for i in range(3))
+        cga[pl.ds(d * gc, gc), :] = one[:gc]
+        cgb[pl.ds(d * gc, gc), :] = one[gc:]
+        wga[pl.ds(d * p, p), :] = two
+        wgb[pl.ds(d * p, p), :] = three
+    wqkv[...] = turned(wqkv_t[...])
+    wproj[...] = turned(wproj_t[...])
+    wdown[...] = turned(wdown_t[...])
+
+
+def unpack_word(all_ref, wqkv_t, wproj_t, wup_t, wdown_t, wqkv, wproj, wup, wdown):
+    nd, nz, rows, lanes = all_ref.shape
+    r = rows // 3
+    a, b = wqkv_t.shape[0] // nd, wproj_t.shape[0] // nd
+    n = r // 2
+    for d in range(nd):
+        t = turned(all_ref[d, :, pl.ds(0, r), :].reshape(nz * r, lanes))
+        wqkv_t[pl.ds(d * a, a), :] = t[:a]
+        wproj_t[pl.ds(d * b, b), :] = t[a:]
+        up = all_ref[d, :, pl.ds(r, r), :].reshape(nz * r, lanes)
+        wup[:, pl.ds(d * lanes, lanes)] = up
+        wup_t[pl.ds(d * lanes, lanes), :] = turned(up)
+        for z in range(nz):
+            for s in range(2):
+                wdown_t[pl.ds(d * n, n), pl.ds((2 * z + s) * lanes, lanes)] = all_ref[
+                    d, z, pl.ds(2 * r + s * n, n), :
+                ]
+    wqkv[...] = turned(wqkv_t[...])
+    wproj[...] = turned(wproj_t[...])
+    wdown[...] = turned(wdown_t[...])
+
+
+def forward_gather_kernel(
+    letters, x_ref, tok_ref, cnt_ref, s_qkv, s_proj, s_up, s_down, s_pool, s_gains, w_qkv, w_proj, w_up, w_down,
+    t_ref, o_ref, p_ref, z1_ref, rs1_ref, z2_ref, rs2_ref, m_ref, gp_ref, pool_ref,
+    word_all, wqkv, wproj, wup, wdown, pool_t, cga, cgb, wga, wgb,
+    char_all, word_own, wqkv_t, wproj_t, wup_t, wdown_t, char_sems, word_sems, own_sem,
+):
+    step = pl.program_id(0)
+    here = place()
+    own = pltpu.make_async_copy(word_own, word_all.at[here], own_sem)
+
+    @pl.when(step == 0)
+    def _():
+        greet()
+        pack_char(char_all.at[here], s_qkv, s_proj, s_up, s_down, s_pool, s_gains)
+        stages = gather_stages(char_all, char_sems)
+        start_all(stages[0])
+        pack_word(word_own, w_qkv, w_proj, w_up, w_down)
+        own.start()
+        for before, after in zip(stages, stages[1:]):
+            arrive_all(before)
+            start_all(after)
+        arrive_all(stages[-1])
+        own.wait()
+        start_all(gather_stages(word_all, word_sems)[0])
+        unpack_char(
+            char_all, wqkv_t, wproj_t, wup_t, wdown_t, wqkv, wproj, wup, wdown, pool_t, cga, cgb, wga, wgb
+        )
+        sent_all(stages)
+
+    for n, when in enumerate((4, 7, 11)):
+        @pl.when(step == when)
+        def _():
+            stages = gather_stages(word_all, word_sems)
+            arrive_all(stages[n])
+            start_all(stages[n + 1])
+
+    char_forward_kernel(
+        letters, x_ref, tok_ref, cnt_ref, cga, cgb, wqkv_t, wproj_t, wup_t, wdown_t,
+        t_ref, o_ref, p_ref, z1_ref, rs1_ref, z2_ref, rs2_ref, m_ref, gp_ref, pool_ref,
+    )
+
+    @pl.when(step == pl.num_programs(0) - 1)
+    def _():
+        stages = gather_stages(word_all, word_sems)
+        arrive_all(stages[-1])
+        sent_all(stages)
+
+
+def forward_gather(x, tok, cnt, char_shards, word_shards, letters):
+    tokens, width = x.shape
+    steps = tokens // STEP
+    nd, nz = lax.axis_size("dp"), lax.axis_size("fsdp")
+    ny, nx, nz = sides()
+    qkv, proj, up, down, pool, gains = char_shards
+    hidden, outer = up.shape[1] * nd, pool.shape[1] * nd
+    per = LANES * letters // STEP
+    word_rows, word_lanes = 3 * word_shards[2].shape[0], word_shards[2].shape[1]
+    char_rows = 4 * up.shape[0]
+
+    def strip(rows, dtype=bf16):
+        return (
+            jax.ShapeDtypeStruct((steps, rows, STEP), dtype),
+            pl.BlockSpec((1, rows, STEP), lambda i: (i, 0, 0)),
+        )
+
+    def whole(shape, dtype=bf16):
+        return (jax.ShapeDtypeStruct(shape, dtype), pl.BlockSpec(shape, lambda i: (0, 0)))
+
+    outs = [
+        strip(3 * width), strip(width), strip(CHAR_HEADS * letters, f32), strip(width), strip(1, f32),
+        strip(width), strip(1, f32), strip(hidden), strip(hidden),
+        (jax.ShapeDtypeStruct((width, tokens // letters), f32), pl.BlockSpec((width, LANES), lambda i: (0, i // per))),
+        (jax.ShapeDtypeStruct((ny, nx, 2, nz, word_rows, word_lanes), bf16), pl.BlockSpec(memory_space=pl.ANY)),
+        whole((width, 3 * width)), whole((width, width)), whole((width, hidden)), whole((hidden, width)),
+        whole((outer, width)), whole((width, LANES), f32), whole((width, LANES), f32),
+        whole((outer, LANES), f32), whole((outer, LANES), f32),
+    ]
+    shards = (*char_shards, *word_shards)
+    return pl.pallas_call(
+        functools.partial(forward_gather_kernel, letters),
+        grid=(steps,),
+        in_specs=[
+            pl.BlockSpec((STEP, width), lambda i: (i, 0)),
+            pl.BlockSpec((1, 1, STEP), lambda i: (i, 0, 0)),
+            pl.BlockSpec((1, LANES), lambda i: (0, i // per)),
+        ] + [full_spec(a) for a in shards],
+        out_specs=[o[1] for o in outs],
+        out_shape=[o[0] for o in outs],
+        scratch_shapes=[
+            pltpu.VMEM((ny, nx, 2, nz, char_rows, LANES), bf16),
+            pltpu.VMEM((word_rows, word_lanes), bf16),
+            pltpu.VMEM((3 * width, width), bf16),
+            pltpu.VMEM((width, width), bf16),
+            pltpu.VMEM((hidden, width), bf16),
+            pltpu.VMEM((width, hidden), bf16),
+            pltpu.SemaphoreType.DMA((2, gather_copies())),
+            pltpu.SemaphoreType.DMA((2, gather_copies())),
+            pltpu.SemaphoreType.DMA,
+        ],
+        compiler_params=pltpu.CompilerParams(
+            dimension_semantics=("arbitrary",), vmem_limit_bytes=56 * 2**20, collective_id=0, has_side_effects=True
+        ),
+        name="forward_gather",
+    )(x, tok, cnt, *shards)
+
+
 def gather_all(shards, counts):
     flat = jnp.concatenate([s.reshape(-1) for s in shards])
     packed = lax.all_gather(lax.all_gather(flat, "fsdp", axis=0), "dp", axis=0)
@@ -477,7 +904,7 @@
     return out
 
 
-def shards(
+def shards_plain(
     characters, counts, separators, cotangent, char_qkv, char_proj, char_up, char_down, char_gain_a, char_gain_b,
     pool_proj, word_qkv, word_proj, word_up, word_down, word_gain_a, word_gain_b,
 ):
@@ -507,6 +934,44 @@
     return (word_out[None], char_grad.reshape(characters.shape), *char_grads, *word_grads)
 
 
+def shards_packed(
+    characters, counts, separators, cotangent, char_qkv, char_proj, char_up, char_down, char_gain_a, char_gain_b,
+    pool_proj, word_qkv, word_proj, word_up, word_down, word_gain_a, word_gain_b,
+):
+    rows, length, letters, width = characters.shape
+    char_shards = (char_qkv, char_proj, char_up, char_down, char_gain_a, char_gain_b)
+    word_shards = (pool_proj, word_qkv, word_proj, word_up, word_down, word_gain_a, word_gain_b)
+    x = characters.reshape(length * letters, width)
+    tok = jnp.repeat(counts, letters, axis=1).reshape(length * letters // STEP, 1, STEP)
+    gains = jnp.concatenate([char_gain_a, char_gain_b, word_gain_a, word_gain_b]).astype(f32).reshape(3, -1)
+    (
+        *saved, pool_sum, word_all, cqkv, cproj, cup, cdown, pool_t, cga, cgb, wga, wgb
+    ) = forward_gather(
+        x, tok, counts, (char_qkv, char_proj, char_up, char_down, pool_proj, gains),
+        (word_qkv, word_proj, word_up, word_down), letters,
+    )
+    word_all = word_all.reshape((-1,) + word_all.shape[3:])
+    word_out, dpool, gpool, gwqkv, gwproj, gwup, gwdown, gwga, gwgb = word_gathered(
+        pool_sum, counts.astype(f32), separators, cotangent.reshape(length, -1), wga, wgb, pool_t, word_all
+    )
+    word_grads = scatter_all(
+        (gpool, gwqkv, gwproj, gwup, gwdown, jnp.sum(gwga, 1), jnp.sum(gwgb, 1)), word_shards
+    )
+    char_grad, gcqkv, gcproj, gcup, gcdown, gcga, gcgb = char_backward(
+        dpool, tok, cga, cgb, cqkv, cproj, cup, cdown, saved, letters
+    )
+    char_grads = scatter_all(
+        (gcqkv, gcproj, gcup, gcdown, jnp.sum(gcga, 1), jnp.sum(gcgb, 1)), char_shards
+    )
+    return (word_out[None], char_grad.reshape(characters.shape), *char_grads, *word_grads)
+
+
+def shards(*arrays):
+    char_qkv, char_proj, word_qkv, word_proj = arrays[4], arrays[5], arrays[11], arrays[12]
+    tiles = (char_qkv.shape[1] + char_proj.shape[1]) // LANES, (word_qkv.shape[1] + word_proj.shape[1]) // LANES
+    return (shards_packed if tiles == (1, 2) else shards_plain)(*arrays)
+
+
 def solution(mesh):
     rows = ("dp", "fsdp")
     matrix, vector = P("fsdp", "dp"), P("dp")

time: 709 us -> 594 us (0.84)
  local copies, waits for them, and re-layouts: 159 us -> 82.6 us
  waiting for transfers between devices: 247 us -> 210 us
  Pallas kernels: 222 us -> 251 us
  blocking collectives: 28.9 us -> 0 us
    reshape x27 -> x0, local copies, waits for them, and re-layouts: 45.7 us -> none  [the longest x11 26.3 us: gather_all(): out.append(piece.reshape(deep_count * r, wide_count * c))]
    unnamed x8 -> x4, waiting for transfers between devices: 247 us -> 210 us
    pallas_call x2, Pallas kernels: 112 us -> 141 us  [the longest x1 109 us: forward_gather(): pl.pallas_call(functools.partial(forward_gather_kernel, letters), grid=(s...]
    all_gather x1 -> x0, blocking collectives: 28.9 us -> none  [gather_all(): packed = lax.all_gather(lax.all_gather(flat, 'fsdp', axis=0), 'dp', axis=0)]
    slice x17 -> x0, local copies, waits for them, and re-layouts: 12.9 us -> none  [gather_all(): piece = packed[:, :, start:start + s.size]]
    unnamed x70 -> x41, local copies, waits for them, and re-layouts: 34.1 us -> 27.5 us
  transfers between devices with their start and end apart: 5 -> 2, of which waited for: 3 -> 2; matrix products, arithmetic and copies ran while one was open for 4% -> 0% of each run, Pallas kernels for 11% -> 0%
where the time goes in v2:
time: 594 us; the launch traced here: 588 us
  Pallas kernels  251 us (42%)
  waiting for transfers between devices  210 us (35%)
  local copies, waits for them, and re-layouts  82.6 us (14%)
  other arithmetic  29.4 us (5%)
  between operations  14.9 us (3%)
    unnamed x4, waiting for transfers between devices  210 us
    pallas_call x1, Pallas kernels, char_backward(): pl.pallas_call(functools.partial(char_backward_kernel, letters), grid=(st...  109 us
    pallas_call x1, Pallas kernels, forward_gather(): pl.pallas_call(functools.partial(forward_gather_kernel, letters), grid=(s...  109 us
    pallas_call x1, Pallas kernels, word_gathered(): pl.pallas_call(word_gathered_kernel, out_shape=[jax.ShapeDtypeStruct((len...  32.8 us
    unnamed x41, local copies, waits for them, and re-layouts  27.5 us
    convert_element_type x9, other arithmetic, scatter_all(): out.append(packed[start:start + s.size].reshape(s.shape).astype(f32))  15.9 us
    reshape x8, local copies, waits for them, and re-layouts, scatter_all(): pieces.append(g.reshape(wide_count, deep_count, s.size))  13.9 us
    concatenate x4, local copies, waits for them, and re-layouts, scatter_all(): packed = jnp.concatenate(pieces, 2)  13.3 us
  transfers between devices with their start and end apart: 2, of which 2 were waited for; matrix products, arithmetic and copies ran while one was open for 0% of the time, Pallas kernels for 0%

profile of v2, /device:TPU:0, one launch (start us, length us, event | category | flops | bytes accessed | tf_op | source)
XLA Modules:
  0.0 587.9 jit_solution(2884710558939178057)
XLA Ops:
  7.7 2.0 fusion.16
  17.9 1.6 copy.75.w_down
  19.5 108.7 %forward_gather.1 = (bf16[16,768,512]{2,1,0:T(8,128)(2,1)}, bf16[16,256,512]{2,1,0:T(8,128)(2,1)}, f32[16,64,512]{2,1,0:T(8,128)}, bf16[16,256,512]{2,1,0:T(8,12...) custom-call(bf16[8192,256]{1,0:T(8,128)(2,1)} %bitcast.95, ...), custom_call_target="tpu_custom_call" | custom-call | tf_op jit(solution)/shard_map/forward_gather/pallas_call | solution.py:841
  128.2 32.8 %word_gathered.1 = (bf16[512,512]{1,0:T(8,128)(2,1)}, bf16[256,512]{1,0:T(8,128)(2,1)}, f32[256,512]{1,0:T(8,128)}, f32[512,1536]{1,0:T(8,128)}, f32[512,512]{1,...) custom-call(f32[256,512]{1,0:T(8,128)} %get-tuple-element.51.pool_sum_ref, ...), custom_call_target="tpu_custom_call" | custom-call | tf_op jit(solution)/shard_map/word_gathered/pallas_call | solution.py:410
  161.0 109.4 %char_backward.1 = (bf16[8192,256]{1,0:T(8,128)(2,1)}, f32[256,768]{1,0:T(8,128)}, f32[256,256]{1,0:T(8,128)}, f32[256,1024]{1,0:T(8,128)}, f32[1024,256]{1,0:T(...) custom-call(bf16[256,512]{1,0:T(8,128)(2,1)} %get-tuple-element.57.dp_ref, s32[16,1,512]{2,1,0:T(1,128)} %broadcast_in_dim.38.tok_ref, ...), custom_call_target="tpu_custom_call" | custom-call | tf_op jit(solution)/shard_map/char_backward/pallas_call | solution.py:277
  277.8 2.3 reshape.208
  282.3 1.8 concatenate.10
  284.1 1.7 copy.82
  288.5 2.1 convert_element_type.179
  291.3 1.9 reshape.211
  293.2 2.9 copy.86
  296.1 3.4 reshape.212
  301.5 2.7 convert_element_type.181
  304.1 2.0 copy.99
  306.4 2.5 copy.89
  309.0 3.3 reshape.217
  312.3 4.3 copy.90
  316.6 5.0 reshape.218
  322.1 2.8 constant_dynamic-update-slice_fusion.3
  330.1 1.6 dynamic-update-slice.6
  331.7 8.1 %copy.91 = bf16[8,4,102528]{2,1,0:T(4,128)(2,1)} copy(bf16[8,4,102528]{2,0,1:T(8,128)(2,1)} %dynamic-update-slice.6) | data formatting | bytes 13123584 | tf_op jit(solution)/shard_map/concatenate | solution.py:897
  341.0 125.0 %all-reduce.9.cloned.1.call-done = (bf16[8,4,24640]{2,1,0:T(4,128)(2,1)}, bf16[8,4,102528]{2,1,0:T(4,128)(2,1)}) async-done(((bf16[8,4,24640]{2,1,0:T(4,128)(2,1)}, bf16[8,4,102528]{2,1,0:T(4,128)(2,1)}), (bf16[8,4,24640]{2,1,0:T(4,128)(2,1)}, bf16[8,4,102528]{2,1,0:T(4,128)(2,1)})) %all-reduce.9.cloned.1.call-update) | async-done | bytes 8138768
  466.0 1.6 constant_dynamic-slice_fusion.5
  468.7 2.1 constant_dynamic-slice_fusion.3
  470.8 2.4 copy.92
  473.9 84.7 %all-reduce.11.cloned.1.call-done = (bf16[1,4,24640]{2,0,1:T(2,128)(2,1)}, bf16[1,4,102528]{2,0,1:T(2,128)(2,1)}) async-done(((bf16[1,4,24640]{2,0,1:T(2,128)(2,1)}, bf16[1,4,102528]{2,0,1:T(2,128)(2,1)}), (bf16[1,4,24640]{2,0,1:T(2,128)(2,1)}, bf16[1,4,102528]{2,0,1:T(2,128)(2,1)})) %all-reduce.11.cloned.1.call-update) | async-done | bytes 1017360
  562.8 2.1 dynamic-slice_convert_fusion.5
  566.3 1.6 fusion.3
  569.4 1.8 fusion.2
  572.9 2.3 fusion
  576.8 1.9 fusion.9
  578.6 1.9 fusion.11
  (95 shorter events, 42.6 us)
Async XLA Ops:
  7.2 458.8 %all-reduce.9.cloned.1.call-start = ((), (), s32[]{:S(2)}) async-start(), calls=%async_computation | async-start | bytes 16285696
  270.4 5.5 copy-start.4
  272.2 3.9 copy-start.3
  293.2 6.3 %copy-start.2 = (f32[512,512]{1,0:T(8,128)S(1)}, f32[512,512]{1,0:T(8,128)}, u32[]{:S(2)}) copy-start(f32[512,512]{1,0:T(8,128)} %get-tuple-element.82) | copy-start | bytes 3145732
  301.5 4.7 copy-start.1
  316.6 5.0 copy-start.6
  316.6 5.3 copy-start.5
  322.1 3.7 copy-start
  339.8 0.7 copy-start.8
  339.8 133.5 %copy-start.7 = (u32[32]{0:T(128)S(1)}, u32[32]{0:T(128)}, u32[]{:S(2)}) copy-start(u32[32]{0:T(128)} %constant.12) | copy-start | bytes 388
  339.8 218.7 %all-reduce.11.cloned.1.call-start = ((), (), s32[]{:S(2)}) async-start(), calls=%async_computation.1 | async-start | bytes 4071424
Sparse Core Ops, SparseCore 0:
  339.9 126.0 all-reduce.8
  473.4 85.1 all-reduce.10

commit v3 on v2

--- a/solution.py
+++ b/solution.py
@@ -248,15 +248,15 @@
         gga_ref[...] += fold_lanes(dy * z)
         dx = dh1 + norm_back(dy, z, rs1_ref[0, :, at], wide(ga_ref[...], SPAN))
         cg_ref[at, :] = dx.T.astype(bf16)
-    gdown_ref[...] += dot_nt(m_ref[0], dh2_ref[...])
+    gdown_ref[...] += dot_nt(dh2_ref[...], m_ref[0])
     gup_ref[...] += dot_nt(z2_ref[0], du_ref[...])
-    gproj_ref[...] += dot_nt(o_ref[0], dh1b_ref[...])
-    gqkv_ref[...] += dot_nt(z1_ref[0], dt_ref[...])
+    gproj_ref[...] += dot_nt(dh1b_ref[...], o_ref[0])
+    gqkv_ref[...] += dot_nt(dt_ref[...], z1_ref[0])
 
     @pl.when(step == pl.num_programs(0) - 1)
     def _():
         gup_ref[...] = gup_ref[...] * wide(gb_ref[...], gup_ref.shape[1])
-        gqkv_ref[...] = gqkv_ref[...] * wide(ga_ref[...], gqkv_ref.shape[1])
+        gqkv_ref[...] = gqkv_ref[...] * ga_ref[...].T[:1]
 
 
 def char_backward(dp, tok, ga, gb, wqkv, wproj, wup, wdown, saved, letters):
@@ -271,7 +271,7 @@
 
     outs = [
         (jax.ShapeDtypeStruct((steps * STEP, width), bf16), pl.BlockSpec((STEP, width), lambda i: (i, 0))),
-        whole((width, 3 * width)), whole((width, width)), whole((width, hidden)), whole((hidden, width)),
+        whole((3 * width, width)), whole((width, width)), whole((width, hidden)), whole((width, hidden)),
         whole((width, LANES)), whole((width, LANES)),
     ]
     return pl.pallas_call(
@@ -300,9 +300,9 @@
 
 def word_gathered_kernel(
     pool_sum_ref, cnt_ref, sep_ref, cot_ref, ga_ref, gb_ref, wpool_t, all_ref,
-    out_ref, dpool_ref, gpool_ref, gqkv_ref, gproj_ref, gup_ref, gdown_ref, gga_ref, ggb_ref,
+    out_ref, dpool_ref, gpool_ref, send_ref, gga_ref, ggb_ref,
     pooled, x, z3, rs3, a3, t, p, o, h3, z4, rs4, a4, m, gp, bias, cot, du, dh3, dh3b, do, dt, dtk,
-    wqkv_t, wproj_t, wup_t, wdown_t, wqkv_ref, wproj_ref, wup_ref, wdown_ref, wpool_ref,
+    wqkv_t, wproj_t, wup_t, wdown_t, wqkv_ref, wproj_ref, wup_ref, wdown_ref, wpool_ref, gqkv_t, gproj_t,
 ):
     unpack_word(all_ref, wqkv_t, wproj_t, wup_t, wdown_t, wqkv_ref, wproj_ref, wup_ref, wdown_ref)
     wpool_ref[...] = turned(wpool_t[...])
@@ -362,9 +362,18 @@
         dh3[:, at] = cot[:, at].astype(f32) + norm_back(dy, z, rs4[:, at], wide(gb_ref[...], SPAN))
         dh3b[:, at] = dh3[:, at].astype(bf16)
         do[:, at] = dot(wproj_ref[...], dh3b[:, at]).astype(bf16)
-    gdown_ref[...] = dot_nt(m[...], cot[...]).astype(gdown_ref.dtype)
-    gup_ref[...] = dot_nt(a4[...], du[...]).astype(gup_ref.dtype)
-    gproj_ref[...] = dot_nt(o[...], dh3b[...]).astype(gproj_ref.dtype)
+    nd, nz, rows, lanes = send_ref.shape
+    r = rows // 3
+    n = r // 2
+    for z in range(nz):
+        for s in range(2):
+            g = dot_nt(cot[...], m[pl.ds((2 * z + s) * lanes, lanes), :]).astype(bf16)
+            for d in range(nd):
+                send_ref[d, z, pl.ds(2 * r + s * n, n), :] = g[d * n : (d + 1) * n]
+    for d in range(nd):
+        g = dot_nt(a4[...], du[pl.ds(d * lanes, lanes), :]).astype(bf16)
+        send_ref[d, :, pl.ds(r, r), :] = g.reshape(nz, r, lanes)
+    gproj_t[...] = dot_nt(dh3b[...], o[...]).astype(bf16)
     for h in range(WORD_HEADS):
         q_rows = pl.ds(h * head, head)
         k_rows = pl.ds(width + h * head, head)
@@ -389,7 +398,13 @@
                 dtk[1, :, keys] += dv
         dt[k_rows, :] = dtk[0].astype(bf16)
         dt[v_rows, :] = dtk[1].astype(bf16)
-    gqkv_ref[...] = dot_nt(a3[...], dt[...]).astype(gqkv_ref.dtype)
+    for n in range(3):
+        part = pl.ds(n * width, width)
+        gqkv_t[part, :] = dot_nt(dt[part, :], a3[...]).astype(bf16)
+    a, b = gqkv_t.shape[0] // nd, gproj_t.shape[0] // nd
+    for d in range(nd):
+        g = turned(jnp.concatenate([gqkv_t[pl.ds(d * a, a), :], gproj_t[pl.ds(d * b, b), :]], 0))
+        send_ref[d, :, pl.ds(0, r), :] = g.reshape(nz, r, lanes)
     for at in halves:
         dy = dot(wqkv_ref[...], dt[:, at])
         z = z3[:, at].astype(f32)
@@ -398,10 +413,10 @@
         dx = dh3[:, at] + norm_back(dy, z, rs3[:, at], wide(ga_ref[...], SPAN))
         dh3b[:, at] = dx.astype(bf16)
         dpool_ref[:, at] = (dot(wpool_ref[...], dh3b[:, at]) / cnt_ref[:, at]).astype(bf16)
-    gpool_ref[...] = dot_nt(pooled[...], dh3b[...]).astype(gpool_ref.dtype)
-
-
-def word_gathered(pool_sum, cnt, sep, cot, ga, gb, pool_t, gathered, grad_type=f32):
+    gpool_ref[...] = dot_nt(dh3b[...], pooled[...])
+
+
+def word_gathered(pool_sum, cnt, sep, cot, ga, gb, pool_t, gathered):
     length, width = cot.shape
     inner = pool_sum.shape[0]
     nd, nz, rows, lanes = gathered.shape
@@ -412,11 +427,8 @@
         out_shape=[
             jax.ShapeDtypeStruct((length, width), bf16),
             jax.ShapeDtypeStruct((inner, length), bf16),
-            jax.ShapeDtypeStruct((inner, width), grad_type),
-            jax.ShapeDtypeStruct((width, 3 * width), grad_type),
-            jax.ShapeDtypeStruct((width, width), grad_type),
-            jax.ShapeDtypeStruct((width, hidden), grad_type),
-            jax.ShapeDtypeStruct((hidden, width), grad_type),
+            jax.ShapeDtypeStruct((width, inner), f32),
+            jax.ShapeDtypeStruct(gathered.shape, bf16),
             jax.ShapeDtypeStruct((width, LANES), f32),
             jax.ShapeDtypeStruct((width, LANES), f32),
         ],
@@ -430,7 +442,7 @@
             vm((3 * width, length), bf16), vm((2, width // WORD_HEADS, length), f32),
             vm((3 * width, width), bf16), vm((width, width), bf16), vm((hidden, width), bf16), vm((width, hidden), bf16),
             vm((width, 3 * width), bf16), vm((width, width), bf16), vm((width, hidden), bf16), vm((hidden, width), bf16),
-            vm((inner, width), bf16),
+            vm((inner, width), bf16), vm((3 * width, width), bf16), vm((width, width), bf16),
         ],
         compiler_params=pltpu.CompilerParams(vmem_limit_bytes=58 * 2**20),
         name="word_gathered",
@@ -615,12 +627,19 @@
     pl.semaphore_wait(barrier, len(partners()))
 
 
+def remote(src, dst, sems, n, other):
+    return pltpu.make_async_remote_copy(
+        src_ref=src, dst_ref=dst, send_sem=sems.at[0, n], recv_sem=sems.at[1, n],
+        device_id=other, device_id_type=MESH,
+    )
+
+
 def gather_copies():
     ny, nx, nz = sides()
     return nz - 1 + 1 + 4 * (nx - 1) + 4 * (ny - 1)
 
 
-def gather_stages(ref, sems):
+def gather_stages(ref, sems, wanted=(0, 1, 2, 3)):
     ny, nx, nz = sides()
     y, x, c, z = place()
     every = slice(None)
@@ -640,15 +659,11 @@
     plan[3] += [((every, (x + k) % nx, c, every, high), twin) for k in range(1, nx)]
     count = 0
     stages = []
-    for part in plan:
+    for n, part in enumerate(plan):
         copies = []
         for where, other in part:
-            copies.append(
-                pltpu.make_async_remote_copy(
-                    src_ref=ref.at[where], dst_ref=ref.at[where], send_sem=sems.at[0, count],
-                    recv_sem=sems.at[1, count], device_id=other, device_id_type=MESH,
-                )
-            )
+            if n in wanted:
+                copies.append(remote(ref.at[where], ref.at[where], sems, count, other))
             count += 1
         stages.append(copies)
     return stages
@@ -783,7 +798,7 @@
             start_all(after)
         arrive_all(stages[-1])
         own.wait()
-        start_all(gather_stages(word_all, word_sems)[0])
+        start_all(gather_stages(word_all, word_sems, (0,))[0])
         unpack_char(
             char_all, wqkv_t, wproj_t, wup_t, wdown_t, wqkv, wproj, wup, wdown, pool_t, cga, cgb, wga, wgb
         )
@@ -792,7 +807,7 @@
     for n, when in enumerate((4, 7, 11)):
         @pl.when(step == when)
         def _():
-            stages = gather_stages(word_all, word_sems)
+            stages = gather_stages(word_all, word_sems, (n, n + 1))
             arrive_all(stages[n])
             start_all(stages[n + 1])
 
@@ -866,6 +881,233 @@
     )(x, tok, cnt, *shards)
 
 
+def scatter_copies():
+    ny, nx, nz = sides()
+    return 1 + 2 * (nx - 1) + 2 * (ny - 1) + nz - 1
+
+
+def scatter_scratch(rows, lanes):
+    ny, nx, nz = sides()
+    half = rows // 2
+    shapes = (
+        (ny, nx, nz, rows, lanes), (ny, nx, nz, rows, lanes), (nx - 1, ny, nz, half, lanes),
+        (ny - 1, nx, nz, half, lanes), (ny - 1, nz, half, lanes), (nx - 1, nz, half, lanes), (nz - 1, rows, lanes),
+    )
+    return [pltpu.VMEM(shape, bf16) for shape in shapes] + [pltpu.SemaphoreType.DMA((2, scatter_copies()))]
+
+
+def scatter_stage(n, send, work):
+    acc, twin_in, one_low, one_high, two_low, two_high, last_in, sems = work
+    ny, nx, nz = sides()
+    y, x, c, z = place()
+    half = acc.shape[3] // 2
+    low, high, every = pl.ds(0, half), pl.ds(half, half), slice(None)
+    plan = [[], [], [], []]
+    plan[0] += [(send, (every, every, 1 - c), twin_in, device(y, x, 1 - c, z))]
+    plan[1] += [
+        (acc, (every, (x + k) % nx, every, low), one_low.at[k - 1], device(y, (x + k) % nx, c, z)) for k in range(1, nx)
+    ]
+    plan[1] += [
+        (acc, ((y + k) % ny, every, every, high), one_high.at[k - 1], device((y + k) % ny, x, c, z)) for k in range(1, ny)
+    ]
+    plan[2] += [
+        (acc, ((y + k) % ny, x, every, low), two_low.at[k - 1], device((y + k) % ny, x, c, z)) for k in range(1, ny)
+    ]
+    plan[2] += [
+        (acc, (y, (x + k) % nx, every, high), two_high.at[k - 1], device(y, (x + k) % nx, c, z)) for k in range(1, nx)
+    ]
+    plan[3] += [(acc, (y, x, (z + k) % nz), last_in.at[k - 1], device(y, x, c, (z + k) % nz)) for k in range(1, nz)]
+    first = sum(len(p) for p in plan[:n])
+    return [remote(src.at[at], dst, sems, first + i, other) for i, (src, at, dst, other) in enumerate(plan[n])]
+
+
+def scatter_sum(n, own, work, out):
+    acc, twin_in, one_low, one_high, two_low, two_high, last_in, sems = work
+    ny, nx, nz = sides()
+    y, x, c, z = place()
+    half = acc.shape[3] // 2
+    low, high = pl.ds(0, half), pl.ds(half, half)
+    if n == 0:
+        for b in range(ny):
+            for a in range(nx):
+                for k in range(nz):
+                    acc[b, a, k] = own(b, a, k) + twin_in[b, a, k]
+    elif n == 1:
+        for k in range(nz):
+            for b in range(ny):
+                acc[b, x, k, low] += sum(one_low[i, b, k] for i in range(nx - 1))
+            for a in range(nx):
+                acc[y, a, k, high] += sum(one_high[i, a, k] for i in range(ny - 1))
+    elif n == 2:
+        for k in range(nz):
+            acc[y, x, k, low] += sum(two_low[i, k] for i in range(ny - 1))
+            acc[y, x, k, high] += sum(two_high[i, k] for i in range(nx - 1))
+    else:
+        out[...] = acc[y, x, z].astype(f32) + sum(last_in[i].astype(f32) for i in range(nz - 1))
+
+
+def pack_char_grads(slots, gqkv_t, gproj_t, gup, gdown_t, gpool_t, gga, ggb, gwga, gwgb):
+    ny, nx, nz = sides()
+    nd = ny * nx * 2
+    r = slots.shape[4] // 4
+    width = nz * r
+    a, b, n, p = (g.shape[0] // nd for g in (gqkv_t, gproj_t, gdown_t, gpool_t))
+    deep = gdown_t.shape[1] // nz
+    gc = gga.shape[0] // nd
+    spot = lax.broadcasted_iota(jnp.int32, (p, width), 1) % r
+    char_a, char_b, word_a, word_b = (jnp.sum(g[...], 1, keepdims=True) for g in (gga, ggb, gwga, gwgb))
+    every = slice(None)
+    for d in range(nd):
+        at = (d // (2 * nx), (d // 2) % nx, d % 2)
+        t = jnp.concatenate([gqkv_t[pl.ds(d * a, a), :], gproj_t[pl.ds(d * b, b), :]], 0)
+        slots[at + (every, pl.ds(0, r))] = t.T.astype(bf16).reshape(nz, r, LANES)
+        slots[at + (every, pl.ds(r, r))] = gup[:, pl.ds(d * LANES, LANES)].astype(bf16).reshape(nz, r, LANES)
+        for z in range(nz):
+            for s in range(2):
+                slots[at + (z, pl.ds(2 * r + s * n, n))] = gdown_t[
+                    pl.ds(d * n, n), pl.ds(z * deep + s * LANES, LANES)
+                ].astype(bf16)
+        both = jnp.concatenate([char_a[d * gc : (d + 1) * gc], char_b[d * gc : (d + 1) * gc]], 0)
+        side = jnp.where(spot == 0, both, 0.0)
+        side = jnp.where(spot == 1, word_a[d * p : (d + 1) * p], side)
+        side = jnp.where(spot == 2, word_b[d * p : (d + 1) * p], side)
+        t = jnp.concatenate([gpool_t[pl.ds(d * p, p), :], side], 0)
+        slots[at + (every, pl.ds(3 * r, r))] = t.T.astype(bf16).reshape(nz, r, LANES)
+
+
+def finish_kernel(
+    char_ref, word_ref, cqkv, cproj, cup, cdown, cga, cgb, pool, wqkv, wproj, wup, wdown, wga, wgb
+):
+    r = cup.shape[0]
+    n = cqkv.shape[1]
+    cqkv[...] = char_ref[pl.ds(0, r), :n]
+    cproj[...] = char_ref[pl.ds(0, r), n:]
+    cup[...] = char_ref[pl.ds(r, r), :]
+    down_t = jnp.concatenate([char_ref[pl.ds(2 * r, r // 2), :], char_ref[pl.ds(2 * r + r // 2, r // 2), :]], 1)
+    cdown[...] = down_t.T
+    p = pool.shape[1]
+    pool[...] = char_ref[pl.ds(3 * r, r), :p]
+    gc = cga.shape[1]
+    side = char_ref[pl.ds(3 * r, 8), :]
+    cga[...] = side[0:1, p : p + gc]
+    cgb[...] = side[0:1, p + gc :]
+    wga[...] = side[1:2, p:]
+    wgb[...] = side[2:3, p:]
+    r = wup.shape[0]
+    n = wqkv.shape[1]
+    wqkv[...] = word_ref[pl.ds(0, r), :n]
+    wproj[...] = word_ref[pl.ds(0, r), n:]
+    wup[...] = word_ref[pl.ds(r, r), :]
+    down_t = jnp.concatenate([word_ref[pl.ds(2 * r, r // 2), :], word_ref[pl.ds(2 * r + r // 2, r // 2), :]], 1)
+    wdown[...] = down_t.T
+
+
+def finish(char_sum, word_sum, like):
+    shapes = [jax.ShapeDtypeStruct(s.shape if s.ndim == 2 else (1, s.shape[0]), f32) for s in like]
+    outs = pl.pallas_call(finish_kernel, out_shape=shapes, name="finish")(char_sum, word_sum)
+    return [o.reshape(s.shape) for o, s in zip(outs, like)]
+
+
+def backward_scatter_kernel(
+    letters, dp_ref, tok_ref, ga_ref, gb_ref, wqkv_ref, wproj_ref, wup_ref, wdown_ref,
+    word_send, gpool_t, gwga, gwgb,
+    t_ref, o_ref, p_ref, z1_ref, rs1_ref, z2_ref, rs2_ref, m_ref, gp_ref,
+    cg_ref, char_out, word_out,
+    dh2_ref, du_ref, dh1b_ref, do_ref, dt_ref, gqkv_ref, gproj_ref, gup_ref, gdown_ref, gga_ref, ggb_ref,
+    own_sem, char_send, *work,
+):
+    step = pl.program_id(0)
+    y, x, c, z = place()
+    word_work, char_work = work[: len(work) // 2], work[len(work) // 2 :]
+    word_acc = word_work[0]
+    own = pltpu.make_async_copy(word_send.at[:, :, c], word_acc, own_sem)
+
+    @pl.when(step == 0)
+    def _():
+        greet()
+        own.start()
+        start_all(scatter_stage(0, word_send, word_work))
+
+    for n, when in enumerate((2, 5, 8, 11)):
+        @pl.when(step == when)
+        def _():
+            arrive_all(scatter_stage(n, word_send, word_work))
+            if n == 0:
+                own.wait()
+            scatter_sum(n, lambda b, a, k: word_acc[b, a, k], word_work, word_out)
+            if n < 3:
+                start_all(scatter_stage(n + 1, word_send, word_work))
+
+    char_backward_kernel(
+        letters, dp_ref, tok_ref, ga_ref, gb_ref, wqkv_ref, wproj_ref, wup_ref, wdown_ref,
+        t_ref, o_ref, p_ref, z1_ref, rs1_ref, z2_ref, rs2_ref, m_ref, gp_ref,
+        cg_ref, gqkv_ref, gproj_ref, gup_ref, gdown_ref, gga_ref, ggb_ref,
+        dh2_ref, du_ref, dh1b_ref, do_ref, dt_ref,
+    )
+
+    @pl.when(step == pl.num_programs(0) - 1)
+    def _():
+        pack_char_grads(char_send, gqkv_ref, gproj_ref, gup_ref, gdown_ref, gpool_t, gga_ref, ggb_ref, gwga, gwgb)
+        for n in range(4):
+            copies = scatter_stage(n, char_send, char_work)
+            start_all(copies)
+            arrive_all(copies)
+            scatter_sum(n, lambda b, a, k: char_send[b, a, c, k], char_work, char_out)
+        for n in range(4):
+            sent_all([scatter_stage(n, char_send, char_work), scatter_stage(n, word_send, word_work)])
+
+
+def backward_scatter(dp, tok, ga, gb, weights, word_send, gpool_t, gwga, gwgb, saved, letters):
+    wqkv, wproj, wup, wdown = weights
+    t = saved[0]
+    steps = t.shape[0]
+    width = wqkv.shape[0]
+    hidden = wup.shape[1]
+    per = LANES * letters // STEP
+    ny, nx, nz = sides()
+    char_rows = 4 * width // nz
+    word_rows, word_lanes = word_send.shape[4:]
+
+    def whole(shape):
+        return (jax.ShapeDtypeStruct(shape, f32), pl.BlockSpec(shape, lambda i: (0, 0)))
+
+    outs = [
+        (jax.ShapeDtypeStruct((steps * STEP, width), bf16), pl.BlockSpec((STEP, width), lambda i: (i, 0))),
+        whole((char_rows, LANES)), whole((word_rows, word_lanes)),
+    ]
+    return pl.pallas_call(
+        functools.partial(backward_scatter_kernel, letters),
+        grid=(steps,),
+        in_specs=[
+            pl.BlockSpec((width, LANES), lambda i: (0, i // per)),
+            pl.BlockSpec((1, 1, STEP), lambda i: (i, 0, 0)),
+        ] + [full_spec(a) for a in (ga, gb, *weights)] + [pl.BlockSpec(memory_space=pl.ANY)]
+        + [full_spec(a) for a in (gpool_t, gwga, gwgb)]
+        + [pl.BlockSpec((1,) + s.shape[1:], lambda i: (i, 0, 0)) for s in saved],
+        out_specs=[o[1] for o in outs],
+        out_shape=[o[0] for o in outs],
+        scratch_shapes=[
+            pltpu.VMEM((width, STEP), bf16),
+            pltpu.VMEM((hidden, STEP), bf16),
+            pltpu.VMEM((width, STEP), bf16),
+            pltpu.VMEM((width, STEP), bf16),
+            pltpu.VMEM((3 * width, STEP), bf16),
+            pltpu.VMEM((3 * width, width), f32),
+            pltpu.VMEM((width, width), f32),
+            pltpu.VMEM((width, hidden), f32),
+            pltpu.VMEM((width, hidden), f32),
+            pltpu.VMEM((width, LANES), f32),
+            pltpu.VMEM((width, LANES), f32),
+            pltpu.SemaphoreType.DMA,
+            pltpu.VMEM((ny, nx, 2, nz, char_rows, LANES), bf16),
+        ] + scatter_scratch(word_rows, word_lanes) + scatter_scratch(char_rows, LANES),
+        compiler_params=pltpu.CompilerParams(
+            dimension_semantics=("arbitrary",), vmem_limit_bytes=58 * 2**20, collective_id=1, has_side_effects=True
+        ),
+        name="backward_scatter",
+    )(dp, tok, ga, gb, *weights, word_send, gpool_t, gwga, gwgb, *saved)
+
+
 def gather_all(shards, counts):
     flat = jnp.concatenate([s.reshape(-1) for s in shards])
     packed = lax.all_gather(lax.all_gather(flat, "fsdp", axis=0), "dp", axis=0)
@@ -939,8 +1181,6 @@
     pool_proj, word_qkv, word_proj, word_up, word_down, word_gain_a, word_gain_b,
 ):
     rows, length, letters, width = characters.shape
-    char_shards = (char_qkv, char_proj, char_up, char_down, char_gain_a, char_gain_b)
-    word_shards = (pool_proj, word_qkv, word_proj, word_up, word_down, word_gain_a, word_gain_b)
     x = characters.reshape(length * letters, width)
     tok = jnp.repeat(counts, letters, axis=1).reshape(length * letters // STEP, 1, STEP)
     gains = jnp.concatenate([char_gain_a, char_gain_b, word_gain_a, word_gain_b]).astype(f32).reshape(3, -1)
@@ -950,20 +1190,19 @@
         x, tok, counts, (char_qkv, char_proj, char_up, char_down, pool_proj, gains),
         (word_qkv, word_proj, word_up, word_down), letters,
     )
-    word_all = word_all.reshape((-1,) + word_all.shape[3:])
-    word_out, dpool, gpool, gwqkv, gwproj, gwup, gwdown, gwga, gwgb = word_gathered(
-        pool_sum, counts.astype(f32), separators, cotangent.reshape(length, -1), wga, wgb, pool_t, word_all
-    )
-    word_grads = scatter_all(
-        (gpool, gwqkv, gwproj, gwup, gwdown, jnp.sum(gwga, 1), jnp.sum(gwgb, 1)), word_shards
-    )
-    char_grad, gcqkv, gcproj, gcup, gcdown, gcga, gcgb = char_backward(
-        dpool, tok, cga, cgb, cqkv, cproj, cup, cdown, saved, letters
-    )
-    char_grads = scatter_all(
-        (gcqkv, gcproj, gcup, gcdown, jnp.sum(gcga, 1), jnp.sum(gcgb, 1)), char_shards
-    )
-    return (word_out[None], char_grad.reshape(characters.shape), *char_grads, *word_grads)
+    word_out, dpool, gpool_t, word_send, gwga, gwgb = word_gathered(
+        pool_sum, counts.astype(f32), separators, cotangent.reshape(length, -1), wga, wgb, pool_t,
+        word_all.reshape((-1,) + word_all.shape[3:]),
+    )
+    char_grad, char_sum, word_sum = backward_scatter(
+        dpool, tok, cga, cgb, (cqkv, cproj, cup, cdown), word_send.reshape(word_all.shape), gpool_t, gwga, gwgb,
+        saved, letters,
+    )
+    like = (
+        char_qkv, char_proj, char_up, char_down, char_gain_a, char_gain_b,
+        pool_proj, word_qkv, word_proj, word_up, word_down, word_gain_a, word_gain_b,
+    )
+    return (word_out[None], char_grad.reshape(characters.shape), *finish(char_sum, word_sum, like))
 
 
 def shards(*arrays):

time: 594 us -> 305 us (0.51)
  waiting for transfers between devices: 210 us -> 0 us
  local copies, waits for them, and re-layouts: 82.6 us -> 21.9 us
  Pallas kernels: 251 us -> 279 us
  other arithmetic: 29.4 us -> 2.77 us
  between operations: 14.9 us -> 0.68 us
    unnamed x4 -> x0, waiting for transfers between devices: 210 us -> none
    pallas_call x1 -> x2, Pallas kernels: 109 us -> 137 us  [the longest x1 135 us: backward_scatter(): pl.pallas_call(functools.partial(backward_scatter_kernel, letters), grid=...]
    convert_element_type x17 -> x0, other arithmetic: 24.3 us -> none  [the longest x9 15.9 us: scatter_all(): out.append(packed[start:start + s.size].reshape(s.shape).astype(f32))]
    reshape x15 -> x0, local copies, waits for them, and re-layouts: 20.6 us -> none  [the longest x8 13.9 us: scatter_all(): pieces.append(g.reshape(wide_count, deep_count, s.size))]
    concatenate x4 -> x0, local copies, waits for them, and re-layouts: 13.3 us -> none  [scatter_all(): packed = jnp.concatenate(pieces, 2)]
    transpose x7 -> x0, local copies, waits for them, and re-layouts: 9.52 us -> none  [scatter_all(): g = g.reshape(deep_count, r, wide_count, c).transpose(2, 0, 1, 3)]
    unnamed x41 -> x12, local copies, waits for them, and re-layouts: 27.5 us -> 20.3 us
    convert_element_type x17 -> x0, local copies, waits for them, and re-layouts: 6.57 us -> none  [the longest x9 4.09 us: scatter_all(): g = g.astype(bf16)]
  transfers between devices with their start and end apart: 2 -> 0, of which waited for: 2 -> 0; matrix products, arithmetic and copies ran while one was open for 0% -> 0% of each run, Pallas kernels for 0% -> 0%
where the time goes in v3:
time: 305 us; the launch traced here: 304 us
  Pallas kernels  279 us (91%)
  local copies, waits for them, and re-layouts  21.9 us (7%)
    pallas_call x1, Pallas kernels, backward_scatter(): pl.pallas_call(functools.partial(backward_scatter_kernel, letters), grid=...  135 us
    pallas_call x1, Pallas kernels, forward_gather(): pl.pallas_call(functools.partial(forward_gather_kernel, letters), grid=(s...  108 us
    pallas_call x1, Pallas kernels, word_gathered(): pl.pallas_call(word_gathered_kernel, out_shape=[jax.ShapeDtypeStruct((len...  33.1 us
    unnamed x12, local copies, waits for them, and re-layouts  20.3 us

profile of v3, /device:TPU:0, one launch (start us, length us, event | category | flops | bytes accessed | tf_op | source)
XLA Modules:
  0.0 304.1 jit_solution(9958814481243862445)
XLA Ops:
  0.6 0.8 maximum_convert_fusion
  1.4 0.7 reshape.80.s_gains
  2.1 0.5 broadcast.9
  2.6 2.0 fusion
  4.6 0.1 broadcast_in_dim.10
  4.7 1.4 copy.43.s_proj
  6.1 1.4 copy.46.w_proj
  7.5 1.4 copy.44.s_down
  8.9 1.5 copy.45.w_qkv
  10.5 1.6 copy.47.w_down
  12.1 0.1 broadcast_in_dim.11
  12.2 0.8 broadcast_in_dim.14.tok_ref
  13.0 108.2 %forward_gather.1 = (bf16[16,768,512]{2,1,0:T(8,128)(2,1)}, bf16[16,256,512]{2,1,0:T(8,128)(2,1)}, f32[16,64,512]{2,1,0:T(8,128)}, bf16[16,256,512]{2,1,0:T(8,12...) custom-call(bf16[8192,256]{1,0:T(8,128)(2,1)} %bitcast.12, ...), custom_call_target="tpu_custom_call" | custom-call | tf_op jit(solution)/shard_map/forward_gather/pallas_call | solution.py:856
  121.2 33.1 %word_gathered.1 = (bf16[512,512]{1,0:T(8,128)(2,1)}, bf16[256,512]{1,0:T(8,128)(2,1)}, f32[512,256]{1,0:T(8,128)}, bf16[8,4,384,256]{3,2,1,0:T(8,128)(2,1)}, f32[512,128]{1,0:T(8,128)}, /*index=5*/f32[512,128]{1,0:T(8,128)}) custom-call(f32[256,512]{1,0:T(8,128)} %get-tuple-element.57.pool_sum_ref, f32[1,512]{1,0:T(1,128)} %get-tuple-element.129.cnt_ref, ...), custom_call_target="tpu_custom_call" | custom-call | tf_op jit(solution)/shard_map/word_gathered/pallas_call | solution.py:425
  154.3 135.2 %backward_scatter.1 = (bf16[8192,256]{1,0:T(8,128)(2,1)}, f32[256,128]{1,0:T(8,128)}, f32[384,256]{1,0:T(8,128)}) custom-call(bf16[256,512]{1,0:T(8,128)(2,1)} %get-tuple-element.63.dp_ref, s32[16,1,512]{2,1,0:T(1,128)} %broadcast_in_dim.14.tok_ref, f32[256,128]{1,0:T(8,128)} %get-tuple-element.64.ga_ref, f32[256,128]{1,0:T(8,128)} %get-tuple-element.65.gb_ref, ...), custom_call_target="tpu_custom_call" | custom-call | tf_op jit(solution)/shard_map/backward_scatter/pallas_call | solution.py:1078
  289.5 2.1 finish.1
  291.7 1.4 copy.49
  293.1 1.6 copy.50
  294.7 1.5 copy.52
  296.2 1.6 copy.51
  297.9 1.7 copy.53
  299.6 4.5 %copy.55 = bf16[1,512,16,256]{3,2,1,0:T(8,128)(2,1)} copy(bf16[1,512,16,256]{3,2,1,0:T(8,128)(2,1)} %bitcast.13) | data formatting | bytes 8388608
